TPU v7x, 256 devices: a whole 4x4x8 slice. The times are simulated.
256 devices in a mesh: acq: 64 (over z, y, core), strip: 4 (over x).
Axes of the slice: x: 4, y: 4, z: 8, core: 2. Of those that a mesh axis runs over, the one named last changes fastest.
Arguments:
- slc_stack: bfloat16 [256, 2, 4, 64, 2048], P('acq', None, 'strip')
- date_pairs: int32 [1024, 2], replicated, may hold values from 0 to 255, as said below
- pair_owner: int32 [1024, 1], replicated, may hold values from 0 to 63; in each aligned block of 1024 rows (0 to 1023, 1024 to 2047, ...) at most 32 rows name the same one
- pseudo_inverse: float32 [256, 1024], replicated, may hold values from -0.1875 to 0.1875
Outputs:
- series_parts: float32 [4, 64, 2, 32, 256], P('strip', 'acq')
- coherence_slots: float32 [2048, 2, 4, 2048], P('acq', None, 'strip')
Inputs may be any that keep to these rules, and one draw needn't show every extreme that they name: `date_pairs`: each pair names two acquisitions, the second later than the first by 1 to 8. `pair_owner`: no owner stores more than 32 pairs; some owner stores exactly 32; every owner stores some.
All inputs are finite; a program needn't handle non-finite values.
Results may differ from a plain program's by a relative error of at most 0.0003.
Values may be sent and summed in bfloat16 or wider, within the bound.
No kernel may reach another device: no remote copies, remote signals or barrier semaphores. Data moves between devices by JAX's collectives and lax.ppermute only.
A program may use at most 128 MiB of HBM per device.

v0:
```python
import jax
import jax.numpy as jnp
from jax import lax
from jax.experimental import pallas as pl
from jax.experimental.pallas import tpu as pltpu
from jax.sharding import PartitionSpec as P

DATES = 256
PAIRS = 1024
OWNERS = 64
CAP = 32
SLOTS = OWNERS * CAP
SPAN = 8
UPPER = 16
LOOKS = 32
LANES = 128
ENTRIES = SPAN * DATES
PLANE = 8
OWN = 4 * PLANE
INNER = OWN - SPAN
TOGETHER = 8
ROWS = CAP // 2 + 1
TABLE = (1 + SPAN // 2) * LANES
VMEM_LIMIT = 20 * 1024 * 1024
F32 = jnp.float32
BF16 = jnp.bfloat16


def dot_nt(left, right):
    return lax.dot_general(
        left, right, (((1,), (1,)), ((), ())), preferred_element_type=F32
    )


def dot_nn(left, right):
    return jnp.dot(left, right, preferred_element_type=F32)


def iota(shape, axis):
    return lax.broadcasted_iota(jnp.int32, shape, axis)


def halves(value):
    high = value.astype(BF16)
    return high, (value - high.astype(F32)).astype(BF16)


def flags(mask):
    return mask.astype(F32).astype(BF16)


def skew_rows(band_ref, dates):
    for start in range(0, band_ref.shape[1], LANES):
        value = band_ref[:, start:start + LANES]
        row = iota(value.shape, 0)
        for bit in (1, 2, 4):
            value = jnp.where((row & bit) != 0, pltpu.roll(value, LANES - bit, 1), value)
        parts = []
        for first in range(0, value.shape[0], 8):
            turn = first % dates
            part = value[first:first + 8]
            parts.append(pltpu.roll(part, LANES - turn, 1) if turn else part)
        band_ref[:, start:start + LANES] = jnp.concatenate(parts, axis=0)


def cell_row(date, kind, u):
    return (u // 4) * 32 + date * 8 + (u % 4) * 2 + kind


def pack_kernel(image_ref, sent_ref, wide_ref):
    blocks = image_ref.shape[1]
    pitch = wide_ref.shape[0] // blocks
    for part in range(8):
        for u in range(UPPER):
            row = cell_row(part // 2, part % 2, u)
            wide_ref[pl.ds(row, blocks, stride=pitch), :] = image_ref[
                part, :, u * LANES:(u + 1) * LANES
            ].astype(F32)
    for block in range(blocks):
        sent_ref[block % PLANE, block // PLANE] = wide_ref[
            block * pitch:block * pitch + LANES, :
        ].astype(BF16)


def slot_kernel(
    mine_ref, dates_ref, owner_ref, pinv_ref,
    code_ref, own_early_ref, own_lag_ref, high_ref, low_ref, table_ref,
):
    owned = iota((OWNERS, PAIRS), 0) == owner_ref[...]
    earlier = flags(iota((PAIRS, PAIRS), 0) < iota((PAIRS, PAIRS), 1))
    before = dot_nn(flags(owned), earlier)
    rank = jnp.sum(jnp.where(owned, before, 0.0), axis=0, keepdims=True)
    slot = owner_ref[...] * CAP + rank.astype(jnp.int32)
    early = dates_ref[0:1, :]
    lag = dates_ref[1:2, :] - early
    entry = (lag - 1) * DATES + early
    numbers = jnp.concatenate(
        [
            jnp.broadcast_to((early + 1).astype(F32), (LANES, PAIRS)),
            jnp.broadcast_to(lag.astype(F32), (LANES, PAIRS)),
        ],
        axis=0,
    ).astype(BF16)
    found = dot_nt(flags(iota((CAP, PAIRS), 0) + mine_ref[0] * CAP == slot), numbers)
    wide = jnp.concatenate([found[:, :LANES], found[:, :LANES]], axis=1)
    own_early_ref[...] = (wide == iota((CAP, DATES), 1).astype(F32) + 1.0).astype(F32)
    own_lag_ref[...] = found[:, LANES:]
    high, low = halves(pinv_ref[...])
    step = 256
    for start in range(0, SLOTS, step):
        rows = slice(start, start + step)
        place = iota((step, PAIRS), 0) + start
        code = dot_nt(numbers, flags(place == slot))
        code_ref[0:8, rows] = code[0:8]
        code_ref[8:16, rows] = code[LANES:LANES + 8]
        chosen = flags(place == entry)
        weight = dot_nt(high, chosen) + dot_nt(low, chosen)
        high_ref[:, rows], low_ref[:, rows] = halves(weight)
    for block in range(8):
        shape = (LANES, TABLE)
        row = iota(shape, 0)
        col = iota(shape, 1)
        inner = row // 16
        look = (block // 2) * 8 + (inner % 4) * 2 + inner // 4
        lag_of = jnp.where(col < LANES, 0, col // (LANES // 2) - 1)
        kind = jnp.where(col < LANES, 0, (col // LOOKS) % 2)
        match = (row % 16 == lag_of) & (col % LOOKS == look) & (kind == block % 2)
        table_ref[block * LANES:(block + 1) * LANES, :] = jnp.where(
            match, 1.0 / 64.0, 0.0
        ).astype(BF16)


def window_masks():
    side_of = (iota((1, 2 * LANES), 1) % 32) // 16
    return [flags(side_of == v) for v in range(2)]


def band_blocks(wide_ref, slot, quarter, dates, keep, store):
    gap = jnp.zeros((LANES // 2 - dates, 2 * LANES), BF16)
    spot = iota((dates, LANES), 1) - (iota((dates, LANES), 0) & -8)
    packed = [None, None]
    for sub in range(4):
        real = wide_ref[slot, pl.ds(2 * sub, dates, stride=8), :]
        imag = wide_ref[slot, pl.ds(2 * sub + 1, dates, stride=8), :]
        straight = jnp.concatenate([real, imag], axis=1).astype(BF16)
        crossed = jnp.concatenate([imag, -real], axis=1).astype(BF16)
        window = jnp.concatenate([straight * keep[0], gap, straight * keep[1], gap], axis=0)
        if sub:
            cut = LANES - 16 * sub
            window = jnp.concatenate([window[cut:], window[:cut]], axis=0)
        gram = dot_nt(jnp.concatenate([straight, crossed], axis=0), window)
        inside = ((spot - 16 * sub) & (LANES // 2 - 1)) < 16
        for kind in range(2):
            part = gram[kind * dates:(kind + 1) * dates]
            packed[kind] = jnp.where(inside, part, packed[kind]) if sub else part
    for kind in range(2):
        store((quarter * 2 + kind) * LANES, packed[kind])


def edge_blocks(wide_ref, slot, quarter, keep, store):
    dates = 2 * SPAN
    straight, crossed = [], []
    for sub in range(4):
        real = wide_ref[slot, pl.ds(2 * sub, dates, stride=8), :]
        imag = wide_ref[slot, pl.ds(2 * sub + 1, dates, stride=8), :]
        straight.append(jnp.concatenate([real, imag], axis=1).astype(BF16))
        crossed.append(jnp.concatenate([imag, -real], axis=1).astype(BF16))
    whole = jnp.concatenate(straight, axis=0)
    window = jnp.concatenate([whole * keep[0], whole * keep[1]], axis=0)
    gram = dot_nt(jnp.concatenate([whole] + crossed, axis=0), window)
    sub_of = (iota((dates, LANES), 1) // 16) % 4
    for kind in range(2):
        value = None
        for sub in range(4):
            start = (kind * 4 + sub) * dates
            part = gram[start:start + dates]
            value = part if value is None else jnp.where(sub_of == sub, part, value)
        store((quarter * 2 + kind) * LANES, value)


def normalised(band_ref, table_ref, scale_ref):
    count = band_ref.shape[0]
    high, low = halves(band_ref[...])
    table = dot_nn(high, table_ref[...]) + dot_nn(low, table_ref[...])
    scale = lax.rsqrt(table[:, :LANES] + 1e-06)
    scale_ref[0:count, :] = scale
    scale_ref[count:count + 8, :] = jnp.zeros((8, LANES), F32)
    left = iota((count, LANES), 1) < LANES // 2
    for pair in range(SPAN // 2):
        lag = 2 * pair + 1
        late = jnp.where(left, scale_ref[lag:lag + count, :], scale_ref[lag + 1:lag + 1 + count, :])
        yield pair, table[:, (pair + 1) * LANES:(pair + 2) * LANES] * scale * late


def window_sums(total):
    pick = flags(iota((8, LANES), 1) // LOOKS == iota((8, LANES), 0))
    high, low = halves(jnp.concatenate([total] * 4, axis=0))
    return (dot_nt(pick, high) + dot_nt(pick, low))[0:4]


def each_tile(tile):
    def body(index, carry):
        for part in range(TOGETHER):
            tile(index * TOGETHER + part, 4 * part)
        return carry

    lax.fori_loop(0, PLANE // TOGETHER, body, 0)


def inner_kernel(
    cells_ref, table_ref, out_ref, sum_ref, table_copy_ref, wide_ref, band_ref, scale_ref
):
    keep = window_masks()

    def tile(index, slot):
        for quarter in range(4):
            rows = slice(quarter * 32, (quarter + 1) * 32)
            wide_ref[slot + quarter] = cells_ref[:, index, rows, :].astype(F32).reshape(OWN * 8, LANES)

            def store(start, value):
                place = pl.ds(pl.multiple_of(index * OWN, OWN), OWN)
                band_ref[place, start:start + LANES] = value

            band_blocks(wide_ref, slot + quarter, quarter, OWN, keep, store)

    each_tile(tile)
    skew_rows(band_ref, OWN)
    table_copy_ref[...] = table_ref[...]
    rest = jnp.zeros((SPAN, LANES), F32)
    for pair, value in normalised(band_ref, table_ref, scale_ref):
        total = jnp.zeros((INNER, LANES), F32)
        for index in range(PLANE):
            part = value[index * OWN:index * OWN + INNER]
            out_ref[index, :, pair * LANES:(pair + 1) * LANES] = part
            total = total + part
        sum_ref[4 * pair:4 * pair + 4, :] = window_sums(jnp.concatenate([total, rest], axis=0))


def edge_kernel(
    cells_ref, halo_ref, table_ref, inner_ref, inner_sum_ref, out_ref, sum_ref,
    wide_ref, band_ref, scale_ref,
):
    keep = window_masks()
    count = 2 * SPAN

    def tile(index, slot):
        for quarter in range(4):
            rows = slice(quarter * 32, (quarter + 1) * 32)
            wide_ref[slot + quarter, 0:SPAN * 8] = (
                cells_ref[:, index, rows, :].astype(F32).reshape(SPAN * 8, LANES)
            )
            wide_ref[slot + quarter, SPAN * 8:] = (
                halo_ref[:, index, rows, :].astype(F32).reshape(SPAN * 8, LANES)
            )

            def store(start, value):
                place = pl.ds(pl.multiple_of(index * count, count), count)
                band_ref[place, start:start + LANES] = value

            edge_blocks(wide_ref, slot + quarter, quarter, keep, store)

    each_tile(tile)
    skew_rows(band_ref, count)
    out_ref[:, 0:INNER, :] = inner_ref[...]
    rest = jnp.zeros((INNER, LANES), F32)
    for pair, value in normalised(band_ref, table_ref, scale_ref):
        total = jnp.zeros((SPAN, LANES), F32)
        for index in range(PLANE):
            part = value[index * count:index * count + SPAN]
            out_ref[index, INNER:, pair * LANES:(pair + 1) * LANES] = part
            total = total + part
        rows = slice(4 * pair, 4 * pair + 4)
        sums = window_sums(jnp.concatenate([rest, total], axis=0))
        sum_ref[rows, :] = inner_sum_ref[rows, :] + sums


def split_table(table_ref):
    left = iota((DATES, LANES), 1) < LANES // 2
    columns = []
    for pair in range(SPAN // 2):
        value = table_ref[:, pair * LANES:(pair + 1) * LANES]
        top = value.astype(BF16).astype(F32)
        rest = pltpu.roll(value - top, LANES // 2, 1)
        columns.append(jnp.where(left, top, rest).astype(BF16))
        columns.append(jnp.where(left, rest, top).astype(BF16))
    return columns


def select_kernel(mine_ref, table_ref, code_ref, sum_ref, send_ref):
    coherence = jnp.concatenate(split_table(table_ref), axis=1)
    wanted = 2 * (mine_ref[0] % PLANE) + iota((2 * SPAN, LANES), 1) // OWN
    extra = jnp.where(iota((2 * SPAN, LANES), 0) == wanted, sum_ref[...], 0.0)
    extra = jnp.sum(extra, axis=0, keepdims=True)
    step = 256
    half = iota((CAP // 2, LANES), 1) < LANES // 2
    column = iota((step, DATES), 1).astype(F32) + 1.0
    for start in range(0, SLOTS, step):
        rows = slice(start, start + step)
        early = jnp.broadcast_to(code_ref[0:1, rows], (LANES, step)).T
        lag_of = jnp.broadcast_to(code_ref[8:9, rows], (LANES, step)).T
        onehot = flags(jnp.concatenate([early, early], axis=1) == column)
        found = dot_nn(onehot, coherence)
        value = jnp.zeros((step, LANES), F32)
        for lag in range(1, SPAN + 1):
            value = jnp.where(lag_of == float(lag), found[:, (lag - 1) * LANES:lag * LANES], value)
        value = value + pltpu.roll(value, LANES // 2, 1)
        for part in range(step // CAP):
            first = part * CAP
            middle = first + CAP // 2
            target = (start // CAP + part) * ROWS
            send_ref[target:target + CAP // 2, :] = jnp.where(
                half, value[first:middle], value[middle:first + CAP]
            )
            send_ref[target + CAP // 2:target + ROWS, :] = extra


def series_kernel(table_ref, high_ref, low_ref, series_ref):
    columns = split_table(table_ref)
    series = jnp.zeros((DATES, LANES), F32)
    for lag in range(SPAN):
        rows = slice(lag * DATES, (lag + 1) * DATES)
        series = series + dot_nn(high_ref[:, rows], columns[lag])
        series = series + dot_nn(low_ref[:, rows], columns[lag])
    series = series + pltpu.roll(series, LANES // 2, 1)
    series_ref[...] = series.T[0:LANES // 2]


def output_kernel(
    got_ref, high_ref, low_ref, own_early_ref, own_lag_ref, series_in_ref, series_ref, slots_ref
):
    sums = got_ref[pl.ds(ROWS - 1, OWNERS, stride=ROWS), :] * (1.0 / 8192.0)
    group = iota((SPAN, LANES), 1) // OWN
    totals = []
    for kind in range(2):
        lanes = []
        for block in range(2):
            value = jnp.zeros((SPAN, LANES), F32)
            for j in range(4):
                plane = block * 4 + j
                part = sums[plane * PLANE:(plane + 1) * PLANE]
                turn = (OWN * (j - kind)) % LANES
                part = pltpu.roll(part, turn, 1) if turn else part
                value = jnp.where(group == j, part, value)
            lanes.append(value)
        totals.append(jnp.concatenate(lanes, axis=1))
    high, low = halves(jnp.concatenate(totals, axis=0))
    lag_of = own_lag_ref[:, 0:1]
    shift = [jnp.zeros((1, DATES), F32) for _ in range(2)]
    found = [jnp.zeros((CAP, DATES), F32) for _ in range(2)]
    for lag in range(SPAN):
        rows = slice(lag * DATES, (lag + 1) * DATES)
        part = (
            dot_nt(high, high_ref[:, rows])
            + dot_nt(low, high_ref[:, rows])
            + dot_nt(high, low_ref[:, rows])
        )
        for kind in range(2):
            row = SPAN * kind + lag
            shift[kind] = shift[kind] + part[row:row + 1]
            found[kind] = jnp.where(
                lag_of == float(lag + 1), totals[kind][lag:lag + 1], found[kind]
            )
    means = []
    for kind in range(2):
        rows = slice(kind * LOOKS, (kind + 1) * LOOKS)
        series_ref[rows, :] = series_in_ref[rows, :] - shift[kind]
        means.append(jnp.sum(found[kind] * own_early_ref[...], axis=1, keepdims=True))
    chunk = iota((CAP // 2, LANES), 1) // LOOKS
    for block in range(OWNERS // 4):
        parts = [
            got_ref[(4 * block + j) * ROWS:(4 * block + j) * ROWS + CAP // 2, :] for j in range(4)
        ]
        for t in range(4):
            side, kind = t // 2, t % 2
            result = None
            for j in range(4):
                turn = (LOOKS * (j - t)) % LANES
                moved = pltpu.roll(parts[j], turn, 1) if turn else parts[j]
                result = moved if result is None else jnp.where(chunk == j, moved, result)
            rows = slice(side * CAP // 2, (side + 1) * CAP // 2)
            first = (side * CAP + kind) * (OWNERS // 4) + block
            slots_ref[pl.ds(first, CAP // 2, stride=OWNERS // 2), :] = result - means[kind][rows]


def vmem(number):
    return [pl.BlockSpec(memory_space=pltpu.VMEM)] * number


def params():
    return pltpu.CompilerParams(vmem_limit_bytes=VMEM_LIMIT)


def cost(flops, size):
    return pl.CostEstimate(flops=flops, bytes_accessed=size, transcendentals=0)


def along(value, axis_groups):
    return lax.all_to_all(
        value, "acq", split_axis=0, concat_axis=0, tiled=True, axis_index_groups=axis_groups
    )


def exchange_sum(value):
    for axis, steps in (("acq", (1,)), ("acq", (2, 4, 6)), ("strip", (1, 2, 3))):
        size = lax.axis_size(axis)
        moved = [
            lax.ppermute(value, axis, [(i, i ^ step) for i in range(size)]) for step in steps
        ]
        for part in moved:
            value = value + part
    return value


SHAPE = jax.ShapeDtypeStruct
SCALAR = [pl.BlockSpec(memory_space=pltpu.SMEM)]


def pack(slc_stack):
    batch = 2 * PLANE
    return pl.pallas_call(
        pack_kernel,
        grid=(OWNERS // batch,),
        out_shape=SHAPE((PLANE, PLANE, LANES, LANES), BF16),
        in_specs=[pl.BlockSpec((8, batch, UPPER * LANES), lambda i: (0, i, 0))],
        out_specs=pl.BlockSpec((PLANE, 2, LANES, LANES), lambda i: (0, i, 0, 0)),
        scratch_shapes=[pltpu.VMEM((batch * (LANES + 4), LANES), F32)],
        compiler_params=params(),
        name="pack",
    )(slc_stack.reshape(8, OWNERS, UPPER * LANES))


def slot_order(mine, date_pairs, pair_owner, pseudo_inverse):
    return pl.pallas_call(
        slot_kernel,
        out_shape=(
            SHAPE((16, SLOTS), F32),
            SHAPE((CAP, DATES), F32),
            SHAPE((CAP, LANES), F32),
            SHAPE((DATES, ENTRIES), BF16),
            SHAPE((DATES, ENTRIES), BF16),
            SHAPE((8 * LANES, TABLE), BF16),
        ),
        in_specs=SCALAR + vmem(3),
        out_specs=tuple(vmem(6)),
        compiler_params=params(),
        name="slot_order",
        cost_estimate=cost(4_000_000_000, 8_000_000),
    )(mine, date_pairs.T, pair_owner.T, pseudo_inverse)


def inner_coherence(cells, table):
    return pl.pallas_call(
        inner_kernel,
        out_shape=(
            SHAPE((PLANE, INNER, SPAN * 2 * LOOKS), F32),
            SHAPE((2 * SPAN, LANES), F32),
            SHAPE(table.shape, BF16),
        ),
        in_specs=vmem(2),
        out_specs=tuple(vmem(3)),
        scratch_shapes=[
            pltpu.VMEM((4 * TOGETHER, OWN * 8, LANES), F32),
            pltpu.VMEM((PLANE * OWN, 8 * LANES), F32),
            pltpu.VMEM((PLANE * OWN + 8, LANES), F32),
        ],
        compiler_params=params(),
        name="coherence",
        cost_estimate=cost(4_000_000_000, 8_000_000),
    )(cells, table)


def edge_coherence(cells, halo, table, inner, inner_sums):
    return pl.pallas_call(
        edge_kernel,
        out_shape=(
            SHAPE((PLANE, OWN, SPAN * 2 * LOOKS), F32),
            SHAPE((2 * SPAN, LANES), F32),
        ),
        in_specs=vmem(5),
        out_specs=tuple(vmem(2)),
        scratch_shapes=[
            pltpu.VMEM((4 * TOGETHER, 2 * SPAN * 8, LANES), F32),
            pltpu.VMEM((PLANE * 2 * SPAN, 8 * LANES), F32),
            pltpu.VMEM((PLANE * 2 * SPAN + 8, LANES), F32),
        ],
        compiler_params=params(),
        name="edge",
        cost_estimate=cost(2_000_000_000, 4_000_000),
    )(cells, halo, table, inner, inner_sums)


def select(mine, coherence, code, sums):
    return pl.pallas_call(
        select_kernel,
        out_shape=SHAPE((OWNERS * ROWS, LANES), F32),
        in_specs=SCALAR + vmem(3),
        out_specs=vmem(1)[0],
        compiler_params=params(),
        name="select",
        cost_estimate=cost(2_000_000_000, 4_000_000),
    )(mine, coherence, code, sums)


def invert(coherence, high, low):
    return pl.pallas_call(
        series_kernel,
        out_shape=SHAPE((2 * LOOKS, DATES), F32),
        in_specs=vmem(3),
        out_specs=vmem(1)[0],
        compiler_params=params(),
        name="series",
        cost_estimate=cost(1_000_000_000, 3_000_000),
    )(coherence, high, low)


def output(got, high, low, own_early, own_lag, series):
    return pl.pallas_call(
        output_kernel,
        out_shape=(SHAPE((2 * LOOKS, DATES), F32), SHAPE((CAP * 2 * UPPER, LANES), F32)),
        in_specs=vmem(6),
        out_specs=tuple(vmem(2)),
        compiler_params=params(),
        name="referenced",
    )(got, high, low, own_early, own_lag, series)


def on_device(slc_stack, date_pairs, pair_owner, pseudo_inverse):
    size = lax.axis_size("acq")
    planes = [list(range(start, start + PLANE)) for start in range(0, size, PLANE)]
    pillars = [list(range(start, size, PLANE)) for start in range(PLANE)]
    mine = lax.axis_index("acq").astype(jnp.int32).reshape(1)
    cells = along(pack(slc_stack), planes)
    ordered = slot_order(mine, date_pairs, pair_owner, pseudo_inverse)
    cells, ordered = lax.optimization_barrier((cells, ordered))
    code, own_early, own_lag, high, low, table = ordered
    halo = lax.ppermute(cells[0:2], "acq", [(i, (i - PLANE) % size) for i in range(size)])
    inner, sums, table = inner_coherence(cells, table)
    parts, sums = edge_coherence(cells[PLANE - 2:], halo, table, inner, sums)
    coherence = along(parts, pillars).reshape(DATES, SPAN * 2 * LOOKS)
    packed = select(mine, coherence, code, exchange_sum(sums))
    got = lax.all_to_all(
        packed.reshape(OWNERS, 1, ROWS * LANES), "acq", split_axis=0, concat_axis=0, tiled=True
    ).reshape(OWNERS * ROWS, LANES)
    series = invert(coherence, high, low)
    series, slots = output(got, high, low, own_early, own_lag, series)
    return (
        series.reshape(1, 1, 2, LOOKS, DATES),
        slots.reshape(CAP, 2, 1, OWNERS * LOOKS),
    )


def solution(mesh):
    placed = (P("acq", None, "strip", None, None), P(), P(), P())
    return jax.shard_map(
        on_device,
        mesh=mesh,
        in_specs=placed,
        out_specs=(P("strip", "acq", None, None, None), P("acq", None, "strip", None)),
        check_vma=False,
    )
```

profile of v0, /device:TPU:1, one launch (start us, length us, event | category | flops | bytes accessed | tf_op | source)
XLA Modules:
  0.0 109.6 jit_solution(5011343953758445774)
XLA Ops:
  0.6 1.6 %copy-done = bf16[4,2,1,64,2048]{4,3,2,1,0:T(8,128)(2,1)S(1)} copy-done((bf16[4,2,1,64,2048]{4,3,2,1,0:T(8,128)(2,1)S(1)}, bf16[4,2,1,64,2048]{4,3,2,1,0:T(8,128)(2,1)}, u32[]{:S(2)}) %copy-start) | copy-done | bytes 2097176
  2.2 2.2 %pack.1 = bf16[8,8,128,128]{3,2,1,0:T(8,128)(2,1)} custom-call(bf16[8,64,2048]{2,1,0:T(8,128)(2,1)S(1)} %bitcast.10), custom_call_target="tpu_custom_call" | custom-call | tf_op jit(solution)/shard_map/pack/pallas_call | solution.py:420
  4.5 6.9 %all-to-all-start = ((bf16[8,8,128,128]{3,2,1,0:T(8,128)(2,1)}), bf16[8,8,128,128]{3,2,1,0:T(8,128)(2,1)S(1)}, u32[]{:S(2)}, u32[]{:S(2)}) async-start(bf16[8,8,128,128]{3,2,1,0:T(8,128)(2,1)} %pack.1), calls=%async_computation | async-start | bytes 4194304 | tf_op jit(solution)/shard_map/all_to_all | solution.py:398
  11.4 1.2 %copy-done.3 = f32[256,1024]{1,0:T(8,128)S(1)} copy-done((f32[256,1024]{1,0:T(8,128)S(1)}, f32[256,1024]{1,0:T(8,128)}, u32[]{:S(2)}) %copy-start.3) | copy-done | bytes 1048600
  12.6 4.2 %slot_order.1 = (f32[16,2048]{1,0:T(8,128)S(1)}, f32[32,256]{1,0:T(8,128)S(1)}, f32[32,128]{1,0:T(8,128)S(1)}, bf16[256,2048]{1,0:T(8,128)(2,1)S(1)}, bf16[256,2...) custom-call(s32[1]{0:T(128)} %bitcast.mine_ref, s32[2,1024]{1,0:T(2,128)S(1)} %bitcast.13, s32[1,1024]{1,0:T(1,128)S(1)} %bitcast.14, ...), custom_call_target="tpu_custom_call" | custom-call | flops 4000000000 | bytes 8000000 | tf_op jit(solution)/shard_map/slot_order/pallas_call | solution.py:433
  16.7 1.0 copy-done.1
  17.7 1.1 copy-done.6
  18.8 18.9 %all-to-all-done.cells_ref = bf16[8,8,128,128]{3,2,1,0:T(8,128)(2,1)S(1)} async-done(((bf16[8,8,128,128]{3,2,1,0:T(8,128)(2,1)}), bf16[8,8,128,128]{3,2,1,0:T(8,128)(2,1)S(1)}, u32[]{:S(2)}, u32[]{:S(2)}) %all-to-all-start) | async-done | bytes 2097184 | tf_op jit(solution)/shard_map/all_to_all | solution.py:398
  37.8 4.9 %collective-permute-start = (bf16[2,8,128,128]{3,2,1,0:T(8,128)(2,1)S(1)}, bf16[2,8,128,128]{3,2,1,0:T(8,128)(2,1)S(1)}, u32[]{:S(2)}, u32[]{:S(2)}) collective-permute-start(bf16[2,8,128,128]{3,2,1,0:T(8,128)(2,1)S(1)} %get-tuple-element.46), channel_id=1, source_target_pairs={{0,224},{4,228},{8,232},{12,236},{16,240},{20,244},{24,248},{28,25... | collective-permute-start | bytes 1572872 | tf_op jit(solution)/shard_map/ppermute | solution.py:536
  42.6 3.9 %coherence.1 = (f32[8,24,512]{2,1,0:T(8,128)S(1)}, f32[16,128]{1,0:T(8,128)S(1)}, bf16[1024,640]{1,0:T(8,128)(2,1)S(1)}) custom-call(bf16[8,8,128,128]{3,2,1,0:T(8,128)(2,1)S(1)} %all-to-all-done.cells_ref, bf16[1024,640]{1,0:T(8,128)(2,1)S(1)} %copy-done.7), custom_call_target="tpu_custom_call" | custom-call | flops 4000000000 | bytes 8000000 | tf_op jit(solution)/shard_map/coherence/pallas_call | solution.py:452
  46.5 6.5 %collective-permute-done.halo_ref = bf16[2,8,128,128]{3,2,1,0:T(8,128)(2,1)S(1)} collective-permute-done((bf16[2,8,128,128]{3,2,1,0:T(8,128)(2,1)S(1)}, bf16[2,8,128,128]{3,2,1,0:T(8,128)(2,1)S(1)}, u32[]{:S(2)}, u32[]{:S(2)}) %collective-permute-start) | collective-permute-done | bytes 524320 | tf_op jit(solution)/shard_map/ppermute | solution.py:536
  53.0 2.6 %edge.1 = (f32[8,32,512]{2,1,0:T(8,128)}, f32[16,128]{1,0:T(8,128)S(1)}) custom-call(bf16[2,8,128,128]{3,2,1,0:T(8,128)(2,1)S(1)} %get-tuple-element.47.cells_ref, bf16[2,8,128,128]{3,2,1,0:T(8,128)(2,1)S(1)} %collective-permute-done.halo_ref, bf16[1024,640]{1,0:T(8,128)(2,1)S(1)} %get-tuple-element.30.table_ref, ...), custom_call_target="tpu_custom_call" | custom-call | flops 2000000000 | bytes 4000000 | tf_op jit(solution)/shard_map/edge/pallas_call | solution.py:473
  55.6 4.8 %all-to-all-start.1 = ((f32[8,32,512]{2,1,0:T(8,128)}), f32[8,32,512]{2,1,0:T(8,128)S(1)}, u32[]{:S(2)}, u32[]{:S(2)}) async-start(f32[8,32,512]{2,1,0:T(8,128)} %get-tuple-element.33), calls=%async_computation.1 | async-start | bytes 1048576 | tf_op jit(solution)/shard_map/all_to_all | solution.py:398
  60.4 2.1 %collective-permute-start.1 = (f32[16,128]{1,0:T(8,128)S(1)}, f32[16,128]{1,0:T(8,128)S(1)}, u32[]{:S(2)}, u32[]{:S(2)}) collective-permute-start(f32[16,128]{1,0:T(8,128)S(1)} %get-tuple-element.35), channel_id=1, source_target_pairs={{0,4},{4,0},{8,12},{12,8},{16,20},{20,16},{24,28},{28,24},{32,36},... | collective-permute-start | bytes 24584 | tf_op jit(solution)/shard_map/ppermute | solution.py:407
  64.2 1.2 %collective-permute-start.3 = (f32[16,128]{1,0:T(8,128)S(1)}, f32[16,128]{1,0:T(8,128)S(1)}, u32[]{:S(2)}, u32[]{:S(2)}) collective-permute-start(f32[16,128]{1,0:T(8,128)S(1)} %add.21), channel_id=1, source_target_pairs={{0,16},{4,20},{8,24},{12,28},{16,0},{20,4},{24,8},{28,12},{32,48},... | collective-permute-start | bytes 24584 | tf_op jit(solution)/shard_map/ppermute | solution.py:407
  65.4 1.2 %collective-permute-start.2 = (f32[16,128]{1,0:T(8,128)S(1)}, f32[16,128]{1,0:T(8,128)S(1)}, u32[]{:S(2)}, u32[]{:S(2)}) collective-permute-start(f32[16,128]{1,0:T(8,128)S(1)} %add.21), channel_id=1, source_target_pairs={{0,8},{4,12},{8,0},{12,4},{16,24},{20,28},{24,16},{28,20},{32,40},... | collective-permute-start | bytes 24584 | tf_op jit(solution)/shard_map/ppermute | solution.py:407
  67.0 1.2 %collective-permute-done.3 = f32[16,128]{1,0:T(8,128)S(1)} collective-permute-done((f32[16,128]{1,0:T(8,128)S(1)}, f32[16,128]{1,0:T(8,128)S(1)}, u32[]{:S(2)}, u32[]{:S(2)}) %collective-permute-start.3) | collective-permute-done | bytes 8224 | tf_op jit(solution)/shard_map/ppermute | solution.py:407
  68.2 2.6 %collective-permute-start.7 = (f32[16,128]{1,0:T(8,128)S(1)}, f32[16,128]{1,0:T(8,128)S(1)}, u32[]{:S(2)}, u32[]{:S(2)}) collective-permute-start(f32[16,128]{1,0:T(8,128)S(1)} %add_add_fusion.1), channel_id=1, source_target_pairs={{0,3},{1,2},{2,1},{3,0},{4,7},{5,6},{6,5},{7,4},{8,11},{9,10},{10,... | collective-permute-start | bytes 24584 | tf_op jit(solution)/shard_map/ppermute | solution.py:407
  72.3 2.5 %collective-permute-done.6 = f32[16,128]{1,0:T(8,128)S(1)} collective-permute-done((f32[16,128]{1,0:T(8,128)S(1)}, f32[16,128]{1,0:T(8,128)S(1)}, u32[]{:S(2)}, u32[]{:S(2)}) %collective-permute-start.6) | collective-permute-done | bytes 8224 | tf_op jit(solution)/shard_map/ppermute | solution.py:407
  74.8 1.3 %all-to-all-done.1 = f32[8,32,512]{2,1,0:T(8,128)S(1)} async-done(((f32[8,32,512]{2,1,0:T(8,128)}), f32[8,32,512]{2,1,0:T(8,128)S(1)}, u32[]{:S(2)}, u32[]{:S(2)}) %all-to-all-start.1) | async-done | bytes 524320 | tf_op jit(solution)/shard_map/all_to_all | solution.py:398
  76.1 2.3 %select.1 = f32[1088,128]{1,0:T(8,128)} custom-call(s32[1]{0:T(128)} %bitcast.mine_ref, f32[256,512]{1,0:T(8,128)S(1)} %bitcast.11, f32[16,2048]{1,0:T(8,128)S(1)} %get-tuple-element.34.code_ref, f32[16,128]{1,0:T(8,128)S(1)} %add_add_fusion.sum_ref), custom_call_target="tpu_custom_call" | custom-call | flops 2000000000 | bytes 4000000 | tf_op jit(solution)/shard_map/select/pallas_call | solution.py:493
  78.5 11.2 %all-to-all-start.2 = ((f32[64,1,2176]{2,1,0:T(1,128)}), f32[64,1,2176]{2,1,0:T(1,128)S(1)}, u32[]{:S(2)}, u32[]{:S(2)}) async-start(f32[64,1,2176]{2,1,0:T(1,128)} %bitcast.5), calls=%async_computation.2 | async-start | bytes 1114112 | tf_op jit(solution)/shard_map/all_to_all | solution.py:541
  90.5 17.5 %all-to-all-done.2 = f32[64,1,2176]{2,1,0:T(1,128)S(1)} async-done(((f32[64,1,2176]{2,1,0:T(1,128)}), f32[64,1,2176]{2,1,0:T(1,128)S(1)}, u32[]{:S(2)}, u32[]{:S(2)}) %all-to-all-start.2) | async-done | bytes 557088 | tf_op jit(solution)/shard_map/all_to_all | solution.py:541
  108.0 1.6 %referenced.1 = (f32[64,256]{1,0:T(8,128)}, f32[1024,128]{1,0:T(8,128)}) custom-call(f32[1088,128]{1,0:T(8,128)S(1)} %bitcast.9, bf16[256,2048]{1,0:T(8,128)(2,1)S(1)} %get-tuple-element.36.high_ref, bf16[256,2048]{1,0:T(8,128)(2,1)S(1)} %copy-done.2, f32[32,256]{1,0:T(8,128)S(1)} %get-tuple-element.38.own_early_ref, ...), custom_call_target="tpu_custom_call" | custom-call | tf_op jit(solution)/shard_map/referenced/pallas_call | solution.py:517
  (25 shorter events, 4.7 us)
Async XLA Ops:
  0.6 1.6 %copy-start = (bf16[4,2,1,64,2048]{4,3,2,1,0:T(8,128)(2,1)S(1)}, bf16[4,2,1,64,2048]{4,3,2,1,0:T(8,128)(2,1)}, u32[]{:S(2)}) copy-start(bf16[4,2,1,64,2048]{4,3,2,1,0:T(8,128)(2,1)} %param.4) | copy-start | bytes 6291460
  4.5 6.9 %copy-start.4 = (s32[1024,2]{0,1:T(2,128)S(1)}, s32[1024,2]{0,1:T(2,128)}, u32[]{:S(2)}) copy-start(s32[1024,2]{0,1:T(2,128)} %param.5) | copy-start | bytes 24580
  4.5 6.9 %copy-start.5 = (s32[1024,1]{0,1:T(1,128)S(1)}, s32[1024,1]{0,1:T(1,128)}, u32[]{:S(2)}) copy-start(s32[1024,1]{0,1:T(1,128)} %param.6) | copy-start | bytes 12292
  4.5 33.2 %all-to-all-start = ((bf16[8,8,128,128]{3,2,1,0:T(8,128)(2,1)}), bf16[8,8,128,128]{3,2,1,0:T(8,128)(2,1)S(1)}, u32[]{:S(2)}, u32[]{:S(2)}) async-start(bf16[8,8,128,128]{3,2,1,0:T(8,128)(2,1)} %pack.1), calls=%async_computation | async-start | bytes 4194304 | tf_op jit(solution)/shard_map/all_to_all | solution.py:398
  11.3 1.2 %copy-start.3 = (f32[256,1024]{1,0:T(8,128)S(1)}, f32[256,1024]{1,0:T(8,128)}, u32[]{:S(2)}) copy-start(f32[256,1024]{1,0:T(8,128)} %pinv_ref.1) | copy-start | bytes 3145732
  16.7 1.0 copy-start.1
  17.7 1.1 copy-start.6
  37.7 5.0 %copy-start.7 = (bf16[1024,640]{1,0:T(8,128)(2,1)S(1)}, bf16[1024,640]{1,0:T(8,128)(2,1)}, u32[]{:S(2)}) copy-start(bf16[1024,640]{1,0:T(8,128)(2,1)} %copy-done.6) | copy-start | bytes 3932164
  37.8 15.2 %collective-permute-start = (bf16[2,8,128,128]{3,2,1,0:T(8,128)(2,1)S(1)}, bf16[2,8,128,128]{3,2,1,0:T(8,128)(2,1)S(1)}, u32[]{:S(2)}, u32[]{:S(2)}) collective-permute-start(bf16[2,8,128,128]{3,2,1,0:T(8,128)(2,1)S(1)} %get-tuple-element.46), channel_id=1, source_target_pairs={{0,224},{4,228},{8,232},{12,236},{16,240},{20,244},{24,248},{28,25... | collective-permute-start | bytes 1572872 | tf_op jit(solution)/shard_map/ppermute | solution.py:536
  55.6 20.5 %all-to-all-start.1 = ((f32[8,32,512]{2,1,0:T(8,128)}), f32[8,32,512]{2,1,0:T(8,128)S(1)}, u32[]{:S(2)}, u32[]{:S(2)}) async-start(f32[8,32,512]{2,1,0:T(8,128)} %get-tuple-element.33), calls=%async_computation.1 | async-start | bytes 1048576 | tf_op jit(solution)/shard_map/all_to_all | solution.py:398
  60.4 2.9 %collective-permute-start.1 = (f32[16,128]{1,0:T(8,128)S(1)}, f32[16,128]{1,0:T(8,128)S(1)}, u32[]{:S(2)}, u32[]{:S(2)}) collective-permute-start(f32[16,128]{1,0:T(8,128)S(1)} %get-tuple-element.35), channel_id=1, source_target_pairs={{0,4},{4,0},{8,12},{12,8},{16,20},{20,16},{24,28},{28,24},{32,36},... | collective-permute-start | bytes 24584 | tf_op jit(solution)/shard_map/ppermute | solution.py:407
  63.3 3.7 %collective-permute-start.4 = (f32[16,128]{1,0:T(8,128)S(1)}, f32[16,128]{1,0:T(8,128)S(1)}, u32[]{:S(2)}, u32[]{:S(2)}) collective-permute-start(f32[16,128]{1,0:T(8,128)S(1)} %add.21), channel_id=1, source_target_pairs={{0,24},{4,28},{8,16},{12,20},{16,8},{20,12},{24,0},{28,4},{32,56},... | collective-permute-start | bytes 24584 | tf_op jit(solution)/shard_map/ppermute | solution.py:407
  64.2 4.0 %collective-permute-start.3 = (f32[16,128]{1,0:T(8,128)S(1)}, f32[16,128]{1,0:T(8,128)S(1)}, u32[]{:S(2)}, u32[]{:S(2)}) collective-permute-start(f32[16,128]{1,0:T(8,128)S(1)} %add.21), channel_id=1, source_target_pairs={{0,16},{4,20},{8,24},{12,28},{16,0},{20,4},{24,8},{28,12},{32,48},... | collective-permute-start | bytes 24584 | tf_op jit(solution)/shard_map/ppermute | solution.py:407
  65.4 2.8 %collective-permute-start.2 = (f32[16,128]{1,0:T(8,128)S(1)}, f32[16,128]{1,0:T(8,128)S(1)}, u32[]{:S(2)}, u32[]{:S(2)}) collective-permute-start(f32[16,128]{1,0:T(8,128)S(1)} %add.21), channel_id=1, source_target_pairs={{0,8},{4,12},{8,0},{12,4},{16,24},{20,28},{24,16},{28,20},{32,40},... | collective-permute-start | bytes 24584 | tf_op jit(solution)/shard_map/ppermute | solution.py:407
  68.2 4.1 %collective-permute-start.7 = (f32[16,128]{1,0:T(8,128)S(1)}, f32[16,128]{1,0:T(8,128)S(1)}, u32[]{:S(2)}, u32[]{:S(2)}) collective-permute-start(f32[16,128]{1,0:T(8,128)S(1)} %add_add_fusion.1), channel_id=1, source_target_pairs={{0,3},{1,2},{2,1},{3,0},{4,7},{5,6},{6,5},{7,4},{8,11},{9,10},{10,... | collective-permute-start | bytes 24584 | tf_op jit(solution)/shard_map/ppermute | solution.py:407
  70.8 4.0 %collective-permute-start.6 = (f32[16,128]{1,0:T(8,128)S(1)}, f32[16,128]{1,0:T(8,128)S(1)}, u32[]{:S(2)}, u32[]{:S(2)}) collective-permute-start(f32[16,128]{1,0:T(8,128)S(1)} %add_add_fusion.1), channel_id=1, source_target_pairs={{0,2},{1,3},{2,0},{3,1},{4,6},{5,7},{6,4},{7,5},{8,10},{9,11},{10,... | collective-permute-start | bytes 24584 | tf_op jit(solution)/shard_map/ppermute | solution.py:407
  71.3 3.5 %collective-permute-start.5 = (f32[16,128]{1,0:T(8,128)S(1)}, f32[16,128]{1,0:T(8,128)S(1)}, u32[]{:S(2)}, u32[]{:S(2)}) collective-permute-start(f32[16,128]{1,0:T(8,128)S(1)} %add_add_fusion.1), channel_id=1, source_target_pairs={{0,1},{1,0},{2,3},{3,2},{4,5},{5,4},{6,7},{7,6},{8,9},{9,8},{10,11... | collective-permute-start | bytes 24584 | tf_op jit(solution)/shard_map/ppermute | solution.py:407
  76.1 13.5 %copy-start.2 = (bf16[256,2048]{1,0:T(8,128)(2,1)S(1)}, bf16[256,2048]{1,0:T(8,128)(2,1)}, u32[]{:S(2)}) copy-start(bf16[256,2048]{1,0:T(8,128)(2,1)} %copy-done.1) | copy-start | bytes 3145732
  78.5 29.5 %all-to-all-start.2 = ((f32[64,1,2176]{2,1,0:T(1,128)}), f32[64,1,2176]{2,1,0:T(1,128)S(1)}, u32[]{:S(2)}, u32[]{:S(2)}) async-start(f32[64,1,2176]{2,1,0:T(1,128)} %bitcast.5), calls=%async_computation.2 | async-start | bytes 1114112 | tf_op jit(solution)/shard_map/all_to_all | solution.py:541
where the time goes:
time: 110 us
  waiting for transfers between devices  49.8 us (45%)
  starting transfers between devices  36.4 us (33%)
  Pallas kernels  17.7 us (16%)
  local copies, waits for them, and re-layouts  4.98 us (5%)
    all_to_all x2, waiting for transfers between devices, along(): lax.all_to_all(value, 'acq', split_axis=0, concat_axis=0, tiled=True, axi...  20.2 us
    all_to_all x1, waiting for transfers between devices, on_device(): lax.all_to_all(packed.reshape(OWNERS, 1, ROWS * LANES), 'acq', split_axis...  17.5 us
    all_to_all x2, starting transfers between devices, along(): lax.all_to_all(value, 'acq', split_axis=0, concat_axis=0, tiled=True, axi...  11.7 us
    all_to_all x1, starting transfers between devices, on_device(): lax.all_to_all(packed.reshape(OWNERS, 1, ROWS * LANES), 'acq', split_axis...  11.2 us
    ppermute x7, starting transfers between devices, exchange_sum(): lax.ppermute(value, axis, [(i, i ^ step) for i in range(size)])  8.65 us
    ppermute x1, waiting for transfers between devices, on_device(): lax.ppermute(cells[0:2], 'acq', [(i, (i - PLANE) % size) for i in range(s...  6.47 us
    ppermute x7, waiting for transfers between devices, exchange_sum(): lax.ppermute(value, axis, [(i, i ^ step) for i in range(size)])  5.7 us
    unnamed x16, local copies, waits for them, and re-layouts  4.9 us
  transfers between devices with their start and end apart: 11, of which 9 were waited for; matrix products, arithmetic and copies ran while one was open for 0% of the time, Pallas kernels for 8%

commit v1 on v0

--- a/solution.py
+++ b/solution.py
@@ -19,9 +19,14 @@
 OWN = 4 * PLANE
 INNER = OWN - SPAN
 TOGETHER = 8
-ROWS = CAP // 2 + 1
+ROWS = CAP // 2 + 2
+PLANE_ORDER = (0, 2, 4, 6, 1, 3, 5, 7)
+PLANE_PLACE = tuple(PLANE_ORDER.index(w) for w in range(PLANE))
+PILLAR_ORDER = (0, 3, 6, 1, 4, 7, 2, 5)
+PILLAR_PLACE = tuple(PILLAR_ORDER.index(z) for z in range(PLANE))
 TABLE = (1 + SPAN // 2) * LANES
 VMEM_LIMIT = 20 * 1024 * 1024
+WIDE_LIMIT = 58 * 1024 * 1024
 F32 = jnp.float32
 BF16 = jnp.bfloat16
 
@@ -67,19 +72,39 @@
     return (u // 4) * 32 + date * 8 + (u % 4) * 2 + kind
 
 
-def pack_kernel(image_ref, sent_ref, wide_ref):
-    blocks = image_ref.shape[1]
-    pitch = wide_ref.shape[0] // blocks
-    for part in range(8):
-        for u in range(UPPER):
-            row = cell_row(part // 2, part % 2, u)
-            wide_ref[pl.ds(row, blocks, stride=pitch), :] = image_ref[
-                part, :, u * LANES:(u + 1) * LANES
-            ].astype(F32)
-    for block in range(blocks):
-        sent_ref[block % PLANE, block // PLANE] = wide_ref[
-            block * pitch:block * pitch + LANES, :
-        ].astype(BF16)
+def pack_kernel(image_ref, sent_ref, held_ref, wide_ref, ready_ref, come_sem, gone_sem):
+    batch = 2 * PLANE
+    pitch = LANES + 4
+    chunks = OWNERS // batch
+    coming, going = [], []
+    for chunk in range(chunks):
+        rows = pl.ds(chunk * batch, batch)
+        copy = pltpu.make_async_copy(
+            image_ref.at[:, rows, :], held_ref.at[:, rows, :], come_sem.at[chunk]
+        )
+        copy.start()
+        coming.append(copy)
+    for chunk in range(chunks):
+        coming[chunk].wait()
+        rows = slice(chunk * batch, (chunk + 1) * batch)
+        for part in range(8):
+            for u in range(UPPER):
+                row = cell_row(part // 2, part % 2, u)
+                wide_ref[chunk % 2, pl.ds(row, batch, stride=pitch), :] = held_ref[
+                    part, rows, u * LANES:(u + 1) * LANES
+                ].astype(F32)
+        for block in range(batch):
+            ready_ref[PLANE_PLACE[block % PLANE], 2 * chunk + block // PLANE] = wide_ref[
+                chunk % 2, block * pitch:block * pitch + LANES, :
+            ].astype(BF16)
+        tiles = pl.ds(2 * chunk, 2)
+        copy = pltpu.make_async_copy(
+            ready_ref.at[:, tiles], sent_ref.at[:, tiles], gone_sem.at[chunk]
+        )
+        copy.start()
+        going.append(copy)
+    for copy in going:
+        copy.wait()
 
 
 def slot_kernel(
@@ -215,7 +240,10 @@
     def tile(index, slot):
         for quarter in range(4):
             rows = slice(quarter * 32, (quarter + 1) * 32)
-            wide_ref[slot + quarter] = cells_ref[:, index, rows, :].astype(F32).reshape(OWN * 8, LANES)
+            for w in range(PLANE):
+                wide_ref[slot + quarter, w * 32:(w + 1) * 32] = cells_ref[
+                    PLANE_PLACE[w], index, rows, :
+                ].astype(F32)
 
             def store(start, value):
                 place = pl.ds(pl.multiple_of(index * OWN, OWN), OWN)
@@ -231,7 +259,7 @@
         total = jnp.zeros((INNER, LANES), F32)
         for index in range(PLANE):
             part = value[index * OWN:index * OWN + INNER]
-            out_ref[index, :, pair * LANES:(pair + 1) * LANES] = part
+            out_ref[PILLAR_PLACE[index], pair * INNER:(pair + 1) * INNER, :] = part
             total = total + part
         sum_ref[4 * pair:4 * pair + 4, :] = window_sums(jnp.concatenate([total, rest], axis=0))
 
@@ -261,13 +289,16 @@
 
     each_tile(tile)
     skew_rows(band_ref, count)
-    out_ref[:, 0:INNER, :] = inner_ref[...]
+    for pair in range(SPAN // 2):
+        out_ref[:, pair * OWN:pair * OWN + INNER, :] = inner_ref[
+            :, pair * INNER:(pair + 1) * INNER, :
+        ]
     rest = jnp.zeros((INNER, LANES), F32)
     for pair, value in normalised(band_ref, table_ref, scale_ref):
         total = jnp.zeros((SPAN, LANES), F32)
         for index in range(PLANE):
             part = value[index * count:index * count + SPAN]
-            out_ref[index, INNER:, pair * LANES:(pair + 1) * LANES] = part
+            out_ref[PILLAR_PLACE[index], pair * OWN + INNER:(pair + 1) * OWN, :] = part
             total = total + part
         rows = slice(4 * pair, 4 * pair + 4)
         sums = window_sums(jnp.concatenate([rest, total], axis=0))
@@ -278,7 +309,8 @@
     left = iota((DATES, LANES), 1) < LANES // 2
     columns = []
     for pair in range(SPAN // 2):
-        value = table_ref[:, pair * LANES:(pair + 1) * LANES]
+        rows = slice(pair * OWN, (pair + 1) * OWN)
+        value = jnp.concatenate([table_ref[place, rows, :] for place in PILLAR_PLACE], axis=0)
         top = value.astype(BF16).astype(F32)
         rest = pltpu.roll(value - top, LANES // 2, 1)
         columns.append(jnp.where(left, top, rest).astype(BF16))
@@ -288,9 +320,12 @@
 
 def select_kernel(mine_ref, table_ref, code_ref, sum_ref, send_ref):
     coherence = jnp.concatenate(split_table(table_ref), axis=1)
-    wanted = 2 * (mine_ref[0] % PLANE) + iota((2 * SPAN, LANES), 1) // OWN
-    extra = jnp.where(iota((2 * SPAN, LANES), 0) == wanted, sum_ref[...], 0.0)
-    extra = jnp.sum(extra, axis=0, keepdims=True)
+    row = iota((2 * SPAN, LANES), 0) - SPAN * (mine_ref[0] % 2)
+    extra = []
+    for part in range(2):
+        wanted = row == 4 * part + iota((2 * SPAN, LANES), 1) // OWN
+        extra.append(jnp.sum(jnp.where(wanted, sum_ref[...], 0.0), axis=0, keepdims=True))
+    extra = jnp.concatenate(extra, axis=0)
     step = 256
     half = iota((CAP // 2, LANES), 1) < LANES // 2
     column = iota((step, DATES), 1).astype(F32) + 1.0
@@ -328,22 +363,25 @@
 def output_kernel(
     got_ref, high_ref, low_ref, own_early_ref, own_lag_ref, series_in_ref, series_ref, slots_ref
 ):
-    sums = got_ref[pl.ds(ROWS - 1, OWNERS, stride=ROWS), :] * (1.0 / 8192.0)
-    group = iota((SPAN, LANES), 1) // OWN
-    totals = []
-    for kind in range(2):
-        lanes = []
-        for block in range(2):
-            value = jnp.zeros((SPAN, LANES), F32)
+    group = iota((PLANE, LANES), 1) // OWN
+    placed = {}
+    for part in range(2):
+        sums = got_ref[pl.ds(CAP // 2 + part, OWNERS, stride=ROWS), :] * (1.0 / 8192.0)
+        for plane in range(PLANE):
+            value = sums[plane * PLANE:(plane + 1) * PLANE]
+            value = value + pltpu.roll(value, 4, 0)
+            value = value + pltpu.roll(value, 2, 0)
             for j in range(4):
-                plane = block * 4 + j
-                part = sums[plane * PLANE:(plane + 1) * PLANE]
-                turn = (OWN * (j - kind)) % LANES
-                part = pltpu.roll(part, turn, 1) if turn else part
-                value = jnp.where(group == j, part, value)
-            lanes.append(value)
-        totals.append(jnp.concatenate(lanes, axis=1))
-    high, low = halves(jnp.concatenate(totals, axis=0))
+                turn = (OWN * (plane - j)) % LANES
+                moved = pltpu.roll(value, turn, 1) if turn else value
+                key = part, j, plane // 4
+                placed[key] = jnp.where(group == plane % 4, moved, placed[key]) if key in placed else moved
+    rows = [
+        jnp.concatenate([placed[part, j, 0], placed[part, j, 1]], axis=1)[core:core + 1]
+        for core in range(2) for part in range(2) for j in range(4)
+    ]
+    total = jnp.concatenate(rows, axis=0)
+    high, low = halves(total)
     lag_of = own_lag_ref[:, 0:1]
     shift = [jnp.zeros((1, DATES), F32) for _ in range(2)]
     found = [jnp.zeros((CAP, DATES), F32) for _ in range(2)]
@@ -355,11 +393,9 @@
             + dot_nt(high, low_ref[:, rows])
         )
         for kind in range(2):
-            row = SPAN * kind + lag
+            row = 2 * lag + kind
             shift[kind] = shift[kind] + part[row:row + 1]
-            found[kind] = jnp.where(
-                lag_of == float(lag + 1), totals[kind][lag:lag + 1], found[kind]
-            )
+            found[kind] = jnp.where(lag_of == float(lag + 1), total[row:row + 1], found[kind])
     means = []
     for kind in range(2):
         rows = slice(kind * LOOKS, (kind + 1) * LOOKS)
@@ -386,8 +422,8 @@
     return [pl.BlockSpec(memory_space=pltpu.VMEM)] * number
 
 
-def params():
-    return pltpu.CompilerParams(vmem_limit_bytes=VMEM_LIMIT)
+def params(limit=VMEM_LIMIT):
+    return pltpu.CompilerParams(vmem_limit_bytes=limit)
 
 
 def cost(flops, size):
@@ -401,7 +437,7 @@
 
 
 def exchange_sum(value):
-    for axis, steps in (("acq", (1,)), ("acq", (2, 4, 6)), ("strip", (1, 2, 3))):
+    for axis, steps in (("acq", (1,)), ("strip", (1, 2, 3))):
         size = lax.axis_size(axis)
         moved = [
             lax.ppermute(value, axis, [(i, i ^ step) for i in range(size)]) for step in steps
@@ -419,12 +455,17 @@
     batch = 2 * PLANE
     return pl.pallas_call(
         pack_kernel,
-        grid=(OWNERS // batch,),
         out_shape=SHAPE((PLANE, PLANE, LANES, LANES), BF16),
-        in_specs=[pl.BlockSpec((8, batch, UPPER * LANES), lambda i: (0, i, 0))],
-        out_specs=pl.BlockSpec((PLANE, 2, LANES, LANES), lambda i: (0, i, 0, 0)),
-        scratch_shapes=[pltpu.VMEM((batch * (LANES + 4), LANES), F32)],
-        compiler_params=params(),
+        in_specs=[pl.BlockSpec(memory_space=pl.ANY)],
+        out_specs=pl.BlockSpec(memory_space=pl.ANY),
+        scratch_shapes=[
+            pltpu.VMEM((8, OWNERS, UPPER * LANES), BF16),
+            pltpu.VMEM((2, batch * (LANES + 4), LANES), F32),
+            pltpu.VMEM((PLANE, PLANE, LANES, LANES), BF16),
+            pltpu.SemaphoreType.DMA((OWNERS // batch,)),
+            pltpu.SemaphoreType.DMA((OWNERS // batch,)),
+        ],
+        compiler_params=params(WIDE_LIMIT),
         name="pack",
     )(slc_stack.reshape(8, OWNERS, UPPER * LANES))
 
@@ -452,7 +493,7 @@
     return pl.pallas_call(
         inner_kernel,
         out_shape=(
-            SHAPE((PLANE, INNER, SPAN * 2 * LOOKS), F32),
+            SHAPE((PLANE, SPAN // 2 * INNER, LANES), F32),
             SHAPE((2 * SPAN, LANES), F32),
             SHAPE(table.shape, BF16),
         ),
@@ -473,7 +514,7 @@
     return pl.pallas_call(
         edge_kernel,
         out_shape=(
-            SHAPE((PLANE, OWN, SPAN * 2 * LOOKS), F32),
+            SHAPE((PLANE, SPAN // 2 * OWN, LANES), F32),
             SHAPE((2 * SPAN, LANES), F32),
         ),
         in_specs=vmem(5),
@@ -507,7 +548,7 @@
         out_shape=SHAPE((2 * LOOKS, DATES), F32),
         in_specs=vmem(3),
         out_specs=vmem(1)[0],
-        compiler_params=params(),
+        compiler_params=params(WIDE_LIMIT),
         name="series",
         cost_estimate=cost(1_000_000_000, 3_000_000),
     )(coherence, high, low)
@@ -526,17 +567,18 @@
 
 def on_device(slc_stack, date_pairs, pair_owner, pseudo_inverse):
     size = lax.axis_size("acq")
-    planes = [list(range(start, start + PLANE)) for start in range(0, size, PLANE)]
-    pillars = [list(range(start, size, PLANE)) for start in range(PLANE)]
+    planes = [[start + w for w in PLANE_ORDER] for start in range(0, size, PLANE)]
+    pillars = [[start + PLANE * z for z in PILLAR_ORDER] for start in range(PLANE)]
     mine = lax.axis_index("acq").astype(jnp.int32).reshape(1)
     cells = along(pack(slc_stack), planes)
     ordered = slot_order(mine, date_pairs, pair_owner, pseudo_inverse)
     cells, ordered = lax.optimization_barrier((cells, ordered))
     code, own_early, own_lag, high, low, table = ordered
-    halo = lax.ppermute(cells[0:2], "acq", [(i, (i - PLANE) % size) for i in range(size)])
+    first, last = (cells[PLANE_PLACE[w]:PLANE:PLANE // 2] for w in (0, PLANE - 2))
+    halo = lax.ppermute(first, "acq", [(i, (i - PLANE) % size) for i in range(size)])
     inner, sums, table = inner_coherence(cells, table)
-    parts, sums = edge_coherence(cells[PLANE - 2:], halo, table, inner, sums)
-    coherence = along(parts, pillars).reshape(DATES, SPAN * 2 * LOOKS)
+    parts, sums = edge_coherence(last, halo, table, inner, sums)
+    coherence = along(parts, pillars)
     packed = select(mine, coherence, code, exchange_sum(sums))
     got = lax.all_to_all(
         packed.reshape(OWNERS, 1, ROWS * LANES), "acq", split_axis=0, concat_axis=0, tiled=True

time: 110 us -> 106 us (0.964)
  starting transfers between devices: 36.4 us -> 28.6 us
  Pallas kernels: 17.7 us -> 20.8 us
  waiting for transfers between devices: 49.8 us -> 51.5 us
    all_to_all x2, waiting for transfers between devices: 20.2 us -> 24.5 us  [along(): lax.all_to_all(value, 'acq', split_axis=0, concat_axis=0, tiled=True, axi...]
    ppermute x7 -> x4, starting transfers between devices: 8.65 us -> 4.72 us  [exchange_sum(): lax.ppermute(value, axis, [(i, i ^ step) for i in range(size)])]
    all_to_all x1, starting transfers between devices: 11.2 us -> 7.29 us  [on_device(): lax.all_to_all(packed.reshape(OWNERS, 1, ROWS * LANES), 'acq', split_axis...]
    pallas_call x1, Pallas kernels: 0.9 us -> 3.37 us  [invert(): pl.pallas_call(series_kernel, out_shape=SHAPE((2 * LOOKS, DATES), F32), i...]
    all_to_all x1, waiting for transfers between devices: 17.5 us -> 15.8 us  [on_device(): lax.all_to_all(packed.reshape(OWNERS, 1, ROWS * LANES), 'acq', split_axis...]
    ppermute x7 -> x4, waiting for transfers between devices: 5.7 us -> 4.2 us  [exchange_sum(): lax.ppermute(value, axis, [(i, i ^ step) for i in range(size)])]
    unnamed x16 -> x22, local copies, waits for them, and re-layouts: 4.9 us -> 3.97 us
  transfers between devices with their start and end apart: 11 -> 8, of which waited for: 9 -> 7; matrix products, arithmetic and copies ran while one was open for 0% -> 0% of each run, Pallas kernels for 8% -> 11%
where the time goes in v1:
time: 106 us
  waiting for transfers between devices  51.5 us (49%)
  starting transfers between devices  28.6 us (27%)
  Pallas kernels  20.8 us (20%)
  local copies, waits for them, and re-layouts  4.05 us (4%)
    all_to_all x2, waiting for transfers between devices, along(): lax.all_to_all(value, 'acq', split_axis=0, concat_axis=0, tiled=True, axi...  24.5 us
    all_to_all x1, waiting for transfers between devices, on_device(): lax.all_to_all(packed.reshape(OWNERS, 1, ROWS * LANES), 'acq', split_axis...  15.8 us
    all_to_all x2, starting transfers between devices, along(): lax.all_to_all(value, 'acq', split_axis=0, concat_axis=0, tiled=True, axi...  11.7 us
    all_to_all x1, starting transfers between devices, on_device(): lax.all_to_all(packed.reshape(OWNERS, 1, ROWS * LANES), 'acq', split_axis...  7.29 us
    ppermute x1, waiting for transfers between devices, on_device(): lax.ppermute(first, 'acq', [(i, (i - PLANE) % size) for i in range(size)])  7.03 us
    ppermute x1, starting transfers between devices, on_device(): lax.ppermute(first, 'acq', [(i, (i - PLANE) % size) for i in range(size)])  4.86 us
    ppermute x4, starting transfers between devices, exchange_sum(): lax.ppermute(value, axis, [(i, i ^ step) for i in range(size)])  4.72 us
    ppermute x4, waiting for transfers between devices, exchange_sum(): lax.ppermute(value, axis, [(i, i ^ step) for i in range(size)])  4.2 us
  transfers between devices with their start and end apart: 8, of which 7 were waited for; matrix products, arithmetic and copies ran while one was open for 0% of the time, Pallas kernels for 11%

profile of v1, /device:TPU:1, one launch (start us, length us, event | category | flops | bytes accessed | tf_op | source)
XLA Modules:
  0.0 105.7 jit_solution(16425181339664123845)
XLA Ops:
  0.6 2.6 %pack.1 = bf16[8,8,128,128]{3,2,1,0:T(8,128)(2,1)} custom-call(bf16[8,64,2048]{2,1,0:T(8,128)(2,1)} %bitcast.11), custom_call_target="tpu_custom_call" | custom-call | tf_op jit(solution)/shard_map/pack/pallas_call | solution.py:456
  3.2 6.9 %all-to-all-start = ((bf16[8,8,128,128]{3,2,1,0:T(8,128)(2,1)}), bf16[8,8,128,128]{3,2,1,0:T(8,128)(2,1)S(1)}, u32[]{:S(2)}, u32[]{:S(2)}) async-start(bf16[8,8,128,128]{3,2,1,0:T(8,128)(2,1)} %pack.1), calls=%async_computation | async-start | bytes 4194304 | tf_op jit(solution)/shard_map/all_to_all | solution.py:434
  10.2 4.2 %slot_order.1 = (f32[16,2048]{1,0:T(8,128)S(1)}, f32[32,256]{1,0:T(8,128)S(1)}, f32[32,128]{1,0:T(8,128)S(1)}, bf16[256,2048]{1,0:T(8,128)(2,1)S(1)}, bf16[256,2...) custom-call(s32[1]{0:T(128)} %bitcast.mine_ref, s32[2,1024]{1,0:T(2,128)S(1)} %bitcast.9, s32[1,1024]{1,0:T(1,128)S(1)} %bitcast.10, ...), custom_call_target="tpu_custom_call" | custom-call | flops 4000000000 | bytes 8000000 | tf_op jit(solution)/shard_map/slot_order/pallas_call | solution.py:474
  14.3 1.0 copy-done
  15.3 1.0 copy-done.2
  16.3 1.1 %copy-done.9 = bf16[1024,640]{1,0:T(8,128)(2,1)} copy-done((bf16[1024,640]{1,0:T(8,128)(2,1)}, bf16[1024,640]{1,0:T(8,128)(2,1)S(1)}, u32[]{:S(2)}) %copy-start.9) | copy-done | bytes 1310744
  17.4 18.9 %all-to-all-done.cells_ref = bf16[8,8,128,128]{3,2,1,0:T(8,128)(2,1)S(1)} async-done(((bf16[8,8,128,128]{3,2,1,0:T(8,128)(2,1)}), bf16[8,8,128,128]{3,2,1,0:T(8,128)(2,1)S(1)}, u32[]{:S(2)}, u32[]{:S(2)}) %all-to-all-start) | async-done | bytes 2097184 | tf_op jit(solution)/shard_map/all_to_all | solution.py:434
  36.5 4.9 %collective-permute-start = (bf16[2,8,128,128]{3,2,1,0:T(8,128)(2,1)S(1)}, bf16[2,8,128,128]{3,2,1,0:T(8,128)(2,1)S(1)}, u32[]{:S(2)}, u32[]{:S(2)}) collective-permute-start(bf16[2,8,128,128]{3,2,1,0:T(8,128)(2,1)S(1)} %get-tuple-element.46), channel_id=1, source_target_pairs={{0,224},{4,228},{8,232},{12,236},{16,240},{20,244},{24,248},{28,25... | collective-permute-start | bytes 1572872 | tf_op jit(solution)/shard_map/ppermute | solution.py:578
  41.3 3.9 %coherence.1 = (f32[8,96,128]{2,1,0:T(8,128)S(1)}, f32[16,128]{1,0:T(8,128)S(1)}, bf16[1024,640]{1,0:T(8,128)(2,1)S(1)}) custom-call(bf16[8,8,128,128]{3,2,1,0:T(8,128)(2,1)S(1)} %all-to-all-done.cells_ref, bf16[1024,640]{1,0:T(8,128)(2,1)S(1)} %copy-done.10), custom_call_target="tpu_custom_call" | custom-call | flops 4000000000 | bytes 8000000 | tf_op jit(solution)/shard_map/coherence/pallas_call | solution.py:493
  45.2 7.0 %collective-permute-done.halo_ref = bf16[2,8,128,128]{3,2,1,0:T(8,128)(2,1)S(1)} collective-permute-done((bf16[2,8,128,128]{3,2,1,0:T(8,128)(2,1)S(1)}, bf16[2,8,128,128]{3,2,1,0:T(8,128)(2,1)S(1)}, u32[]{:S(2)}, u32[]{:S(2)}) %collective-permute-start) | collective-permute-done | bytes 524320 | tf_op jit(solution)/shard_map/ppermute | solution.py:578
  52.3 2.6 %edge.1 = (f32[8,128,128]{2,1,0:T(8,128)}, f32[16,128]{1,0:T(8,128)S(1)}) custom-call(bf16[2,8,128,128]{3,2,1,0:T(8,128)(2,1)S(1)} %get-tuple-element.47.cells_ref, bf16[2,8,128,128]{3,2,1,0:T(8,128)(2,1)S(1)} %collective-permute-done.halo_ref, bf16[1024,640]{1,0:T(8,128)(2,1)S(1)} %get-tuple-element.30.table_ref, ...), custom_call_target="tpu_custom_call" | custom-call | flops 2000000000 | bytes 4000000 | tf_op jit(solution)/shard_map/edge/pallas_call | solution.py:514
  54.9 4.8 %all-to-all-start.1 = ((f32[8,128,128]{2,1,0:T(8,128)}), f32[8,128,128]{2,1,0:T(8,128)S(1)}, u32[]{:S(2)}, u32[]{:S(2)}) async-start(f32[8,128,128]{2,1,0:T(8,128)} %get-tuple-element.33), calls=%async_computation.1 | async-start | bytes 1048576 | tf_op jit(solution)/shard_map/all_to_all | solution.py:434
  59.7 1.5 %collective-permute-start.1 = (f32[16,128]{1,0:T(8,128)S(1)}, f32[16,128]{1,0:T(8,128)S(1)}, u32[]{:S(2)}, u32[]{:S(2)}) collective-permute-start(f32[16,128]{1,0:T(8,128)S(1)} %get-tuple-element.35), channel_id=1, source_target_pairs={{0,4},{4,0},{8,12},{12,8},{16,20},{20,16},{24,28},{28,24},{32,36},... | collective-permute-start | bytes 24584 | tf_op jit(solution)/shard_map/ppermute | solution.py:443
  61.1 0.8 collective-permute-done.1
  62.0 2.5 %collective-permute-start.4 = (f32[16,128]{1,0:T(8,128)S(1)}, f32[16,128]{1,0:T(8,128)S(1)}, u32[]{:S(2)}, u32[]{:S(2)}) collective-permute-start(f32[16,128]{1,0:T(8,128)S(1)} %add.12), channel_id=1, source_target_pairs={{0,3},{1,2},{2,1},{3,0},{4,7},{5,6},{6,5},{7,4},{8,11},{9,10},{10,... | collective-permute-start | bytes 24584 | tf_op jit(solution)/shard_map/ppermute | solution.py:443
  64.5 0.5 collective-permute-start.3
  65.7 2.9 %collective-permute-done.3 = f32[16,128]{1,0:T(8,128)S(1)} collective-permute-done((f32[16,128]{1,0:T(8,128)S(1)}, f32[16,128]{1,0:T(8,128)S(1)}, u32[]{:S(2)}, u32[]{:S(2)}) %collective-permute-start.3) | collective-permute-done | bytes 8224 | tf_op jit(solution)/shard_map/ppermute | solution.py:443
  68.6 5.6 %all-to-all-done.1.table_ref = f32[8,128,128]{2,1,0:T(8,128)S(1)} async-done(((f32[8,128,128]{2,1,0:T(8,128)}), f32[8,128,128]{2,1,0:T(8,128)S(1)}, u32[]{:S(2)}, u32[]{:S(2)}) %all-to-all-start.1) | async-done | bytes 524320 | tf_op jit(solution)/shard_map/all_to_all | solution.py:434
  74.2 2.4 %select.1 = f32[1152,128]{1,0:T(8,128)} custom-call(s32[1]{0:T(128)} %bitcast.mine_ref, f32[8,128,128]{2,1,0:T(8,128)S(1)} %all-to-all-done.1.table_ref, f32[16,2048]{1,0:T(8,128)S(1)} %get-tuple-element.34.code_ref, f32[16,128]{1,0:T(8,128)S(1)} %add_add_fusion.sum_ref), custom_call_target="tpu_custom_call" | custom-call | flops 2000000000 | bytes 4000000 | tf_op jit(solution)/shard_map/select/pallas_call | solution.py:534
  76.6 7.3 %all-to-all-start.2 = ((f32[64,1,2304]{2,1,0:T(1,128)}), f32[64,1,2304]{2,1,0:T(1,128)S(1)}, u32[]{:S(2)}, u32[]{:S(2)}) async-start(f32[64,1,2304]{2,1,0:T(1,128)} %bitcast.4), calls=%async_computation.2 | async-start | bytes 1179648 | tf_op jit(solution)/shard_map/all_to_all | solution.py:583
  83.9 3.4 %series.1.series_in_ref = f32[64,256]{1,0:T(8,128)} custom-call(f32[8,128,128]{2,1,0:T(8,128)} %copy-done.4, bf16[256,2048]{1,0:T(8,128)(2,1)} %copy-done, bf16[256,2048]{1,0:T(8,128)(2,1)} %copy-done.2), custom_call_target="tpu_custom_call" | custom-call | flops 1000000000 | bytes 3000000 | tf_op jit(solution)/shard_map/series/pallas_call | solution.py:546
  87.3 15.8 %all-to-all-done.2 = f32[64,1,2304]{2,1,0:T(1,128)S(1)} async-done(((f32[64,1,2304]{2,1,0:T(1,128)}), f32[64,1,2304]{2,1,0:T(1,128)S(1)}, u32[]{:S(2)}, u32[]{:S(2)}) %all-to-all-start.2) | async-done | bytes 589856 | tf_op jit(solution)/shard_map/all_to_all | solution.py:583
  103.1 0.8 copy-done.5
  103.9 1.8 %referenced.1 = (f32[64,256]{1,0:T(8,128)}, f32[1024,128]{1,0:T(8,128)}) custom-call(f32[1152,128]{1,0:T(8,128)S(1)} %bitcast.8, bf16[256,2048]{1,0:T(8,128)(2,1)S(1)} %copy-done.1, bf16[256,2048]{1,0:T(8,128)(2,1)S(1)} %copy-done.3, f32[32,256]{1,0:T(8,128)S(1)} %get-tuple-element.38.own_early_ref, f32[32,128]{1,0:T(8,128)S(1)} %get-tuple-element.39.own_lag_ref, ...), custom_call_target="tpu_custom_call" | custom-call | tf_op jit(solution)/shard_map/referenced/pallas_call | solution.py:558
  (24 shorter events, 0.8 us)
Async XLA Ops:
  3.2 6.9 %copy-start.6 = (f32[256,1024]{1,0:T(8,128)S(1)}, f32[256,1024]{1,0:T(8,128)}, u32[]{:S(2)}) copy-start(f32[256,1024]{1,0:T(8,128)} %pinv_ref.1) | copy-start | bytes 3145732
  3.2 6.9 %copy-start.7 = (s32[1024,2]{0,1:T(2,128)S(1)}, s32[1024,2]{0,1:T(2,128)}, u32[]{:S(2)}) copy-start(s32[1024,2]{0,1:T(2,128)} %param.5) | copy-start | bytes 24580
  3.2 6.9 %copy-start.8 = (s32[1024,1]{0,1:T(1,128)S(1)}, s32[1024,1]{0,1:T(1,128)}, u32[]{:S(2)}) copy-start(s32[1024,1]{0,1:T(1,128)} %param.6) | copy-start | bytes 12292
  3.2 33.1 %all-to-all-start = ((bf16[8,8,128,128]{3,2,1,0:T(8,128)(2,1)}), bf16[8,8,128,128]{3,2,1,0:T(8,128)(2,1)S(1)}, u32[]{:S(2)}, u32[]{:S(2)}) async-start(bf16[8,8,128,128]{3,2,1,0:T(8,128)(2,1)} %pack.1), calls=%async_computation | async-start | bytes 4194304 | tf_op jit(solution)/shard_map/all_to_all | solution.py:434
  14.3 1.0 copy-start
  15.3 1.0 copy-start.2
  16.3 1.1 %copy-start.9 = (bf16[1024,640]{1,0:T(8,128)(2,1)}, bf16[1024,640]{1,0:T(8,128)(2,1)S(1)}, u32[]{:S(2)}) copy-start(bf16[1024,640]{1,0:T(8,128)(2,1)S(1)} %get-tuple-element.29.table_ref) | copy-start | bytes 3932164
  36.4 4.9 %copy-start.10 = (bf16[1024,640]{1,0:T(8,128)(2,1)S(1)}, bf16[1024,640]{1,0:T(8,128)(2,1)}, u32[]{:S(2)}) copy-start(bf16[1024,640]{1,0:T(8,128)(2,1)} %copy-done.9) | copy-start | bytes 3932164
  36.5 15.8 %collective-permute-start = (bf16[2,8,128,128]{3,2,1,0:T(8,128)(2,1)S(1)}, bf16[2,8,128,128]{3,2,1,0:T(8,128)(2,1)S(1)}, u32[]{:S(2)}, u32[]{:S(2)}) collective-permute-start(bf16[2,8,128,128]{3,2,1,0:T(8,128)(2,1)S(1)} %get-tuple-element.46), channel_id=1, source_target_pairs={{0,224},{4,228},{8,232},{12,236},{16,240},{20,244},{24,248},{28,25... | collective-permute-start | bytes 1572872 | tf_op jit(solution)/shard_map/ppermute | solution.py:578
  54.9 19.3 %all-to-all-start.1 = ((f32[8,128,128]{2,1,0:T(8,128)}), f32[8,128,128]{2,1,0:T(8,128)S(1)}, u32[]{:S(2)}, u32[]{:S(2)}) async-start(f32[8,128,128]{2,1,0:T(8,128)} %get-tuple-element.33), calls=%async_computation.1 | async-start | bytes 1048576 | tf_op jit(solution)/shard_map/all_to_all | solution.py:434
  59.7 2.3 %collective-permute-start.1 = (f32[16,128]{1,0:T(8,128)S(1)}, f32[16,128]{1,0:T(8,128)S(1)}, u32[]{:S(2)}, u32[]{:S(2)}) collective-permute-start(f32[16,128]{1,0:T(8,128)S(1)} %get-tuple-element.35), channel_id=1, source_target_pairs={{0,4},{4,0},{8,12},{12,8},{16,20},{20,16},{24,28},{28,24},{32,36},... | collective-permute-start | bytes 24584 | tf_op jit(solution)/shard_map/ppermute | solution.py:443
  62.0 3.7 %collective-permute-start.4 = (f32[16,128]{1,0:T(8,128)S(1)}, f32[16,128]{1,0:T(8,128)S(1)}, u32[]{:S(2)}, u32[]{:S(2)}) collective-permute-start(f32[16,128]{1,0:T(8,128)S(1)} %add.12), channel_id=1, source_target_pairs={{0,3},{1,2},{2,1},{3,0},{4,7},{5,6},{6,5},{7,4},{8,11},{9,10},{10,... | collective-permute-start | bytes 24584 | tf_op jit(solution)/shard_map/ppermute | solution.py:443
  64.5 4.1 %collective-permute-start.3 = (f32[16,128]{1,0:T(8,128)S(1)}, f32[16,128]{1,0:T(8,128)S(1)}, u32[]{:S(2)}, u32[]{:S(2)}) collective-permute-start(f32[16,128]{1,0:T(8,128)S(1)} %add.12), channel_id=1, source_target_pairs={{0,2},{1,3},{2,0},{3,1},{4,6},{5,7},{6,4},{7,5},{8,10},{9,11},{10,... | collective-permute-start | bytes 24584 | tf_op jit(solution)/shard_map/ppermute | solution.py:443
  65.0 3.6 %collective-permute-start.2 = (f32[16,128]{1,0:T(8,128)S(1)}, f32[16,128]{1,0:T(8,128)S(1)}, u32[]{:S(2)}, u32[]{:S(2)}) collective-permute-start(f32[16,128]{1,0:T(8,128)S(1)} %add.12), channel_id=1, source_target_pairs={{0,1},{1,0},{2,3},{3,2},{4,5},{5,4},{6,7},{7,6},{8,9},{9,8},{10,11... | collective-permute-start | bytes 24584 | tf_op jit(solution)/shard_map/ppermute | solution.py:443
  74.2 2.4 %copy-start.4 = (f32[8,128,128]{2,1,0:T(8,128)}, f32[8,128,128]{2,1,0:T(8,128)S(1)}, u32[]{:S(2)}) copy-start(f32[8,128,128]{2,1,0:T(8,128)S(1)} %all-to-all-done.1.table_ref) | copy-start | bytes 1572868
  76.6 26.5 %all-to-all-start.2 = ((f32[64,1,2304]{2,1,0:T(1,128)}), f32[64,1,2304]{2,1,0:T(1,128)S(1)}, u32[]{:S(2)}, u32[]{:S(2)}) async-start(f32[64,1,2304]{2,1,0:T(1,128)} %bitcast.4), calls=%async_computation.2 | async-start | bytes 1179648 | tf_op jit(solution)/shard_map/all_to_all | solution.py:583
  83.9 19.2 %copy-start.1 = (bf16[256,2048]{1,0:T(8,128)(2,1)S(1)}, bf16[256,2048]{1,0:T(8,128)(2,1)}, u32[]{:S(2)}) copy-start(bf16[256,2048]{1,0:T(8,128)(2,1)} %copy-done) | copy-start | bytes 3145732
  83.9 19.2 %copy-start.3 = (bf16[256,2048]{1,0:T(8,128)(2,1)S(1)}, bf16[256,2048]{1,0:T(8,128)(2,1)}, u32[]{:S(2)}) copy-start(bf16[256,2048]{1,0:T(8,128)(2,1)} %copy-done.2) | copy-start | bytes 3145732
  103.0 0.8 copy-start.5

commit v2 on v1

--- a/solution.py
+++ b/solution.py
@@ -19,7 +19,8 @@
 OWN = 4 * PLANE
 INNER = OWN - SPAN
 TOGETHER = 8
-ROWS = CAP // 2 + 2
+ROWS = CAP // 2 + 3
+HALF = PLANE // 2
 PLANE_ORDER = (0, 2, 4, 6, 1, 3, 5, 7)
 PLANE_PLACE = tuple(PLANE_ORDER.index(w) for w in range(PLANE))
 PILLAR_ORDER = (0, 3, 6, 1, 4, 7, 2, 5)
@@ -219,7 +220,7 @@
 
 def window_sums(total):
     pick = flags(iota((8, LANES), 1) // LOOKS == iota((8, LANES), 0))
-    high, low = halves(jnp.concatenate([total] * 4, axis=0))
+    high, low = halves(jnp.concatenate([total] * (LANES // total.shape[0]), axis=0))
     return (dot_nt(pick, high) + dot_nt(pick, low))[0:4]
 
 
@@ -265,52 +266,56 @@
 
 
 def edge_kernel(
-    cells_ref, halo_ref, table_ref, inner_ref, inner_sum_ref, out_ref, sum_ref,
-    wide_ref, band_ref, scale_ref,
+    last_ref, next_ref, before_ref, first_ref, table_ref, inner_ref, inner_sum_ref,
+    out_ref, sum_ref, wide_ref, band_ref, scale_ref,
 ):
     keep = window_masks()
     count = 2 * SPAN
-
-    def tile(index, slot):
+    for index in range(PLANE):
+        early_ref, late_ref = (last_ref, next_ref) if index < HALF else (before_ref, first_ref)
         for quarter in range(4):
+            slot = 4 * index + quarter
             rows = slice(quarter * 32, (quarter + 1) * 32)
-            wide_ref[slot + quarter, 0:SPAN * 8] = (
-                cells_ref[:, index, rows, :].astype(F32).reshape(SPAN * 8, LANES)
-            )
-            wide_ref[slot + quarter, SPAN * 8:] = (
-                halo_ref[:, index, rows, :].astype(F32).reshape(SPAN * 8, LANES)
-            )
+            for part, source in enumerate((early_ref, late_ref)):
+                wide_ref[slot, part * SPAN * 8:(part + 1) * SPAN * 8] = (
+                    source[:, index % HALF, rows, :].astype(F32).reshape(SPAN * 8, LANES)
+                )
 
             def store(start, value):
-                place = pl.ds(pl.multiple_of(index * count, count), count)
-                band_ref[place, start:start + LANES] = value
-
-            edge_blocks(wide_ref, slot + quarter, quarter, keep, store)
-
-    each_tile(tile)
+                band_ref[index * count:(index + 1) * count, start:start + LANES] = value
+
+            edge_blocks(wide_ref, slot, quarter, keep, store)
     skew_rows(band_ref, count)
-    for pair in range(SPAN // 2):
+    rest = jnp.zeros((INNER, LANES), F32)
+    for pair, value in normalised(band_ref, table_ref, scale_ref):
+        totals = [jnp.zeros((SPAN, LANES), F32), jnp.zeros((SPAN, LANES), F32)]
+        for index in range(PLANE):
+            part = value[index * count:index * count + SPAN]
+            out_ref[PILLAR_PLACE[index], pair * OWN + INNER:(pair + 1) * OWN, :] = part
+            totals[index // HALF] = totals[index // HALF] + part
         out_ref[:, pair * OWN:pair * OWN + INNER, :] = inner_ref[
             :, pair * INNER:(pair + 1) * INNER, :
         ]
-    rest = jnp.zeros((INNER, LANES), F32)
-    for pair, value in normalised(band_ref, table_ref, scale_ref):
-        total = jnp.zeros((SPAN, LANES), F32)
-        for index in range(PLANE):
-            part = value[index * count:index * count + SPAN]
-            out_ref[PILLAR_PLACE[index], pair * OWN + INNER:(pair + 1) * OWN, :] = part
-            total = total + part
         rows = slice(4 * pair, 4 * pair + 4)
-        sums = window_sums(jnp.concatenate([rest, total], axis=0))
+        sums = window_sums(jnp.concatenate([rest, totals[0]], axis=0))
         sum_ref[rows, :] = inner_sum_ref[rows, :] + sums
-
-
-def split_table(table_ref):
+        sum_ref[2 * SPAN + 4 * pair:2 * SPAN + 4 * pair + 4, :] = window_sums(totals[1])
+
+
+def split_table(mine_ref, table_ref):
+    upper = mine_ref[0] // PLANE >= HALF
     left = iota((DATES, LANES), 1) < LANES // 2
     columns = []
     for pair in range(SPAN // 2):
-        rows = slice(pair * OWN, (pair + 1) * OWN)
-        value = jnp.concatenate([table_ref[place, rows, :] for place in PILLAR_PLACE], axis=0)
+        inner = slice(pair * OWN, pair * OWN + INNER)
+        edge = slice(pair * OWN + INNER, (pair + 1) * OWN)
+        parts = []
+        for plane in range(PLANE):
+            parts.append(table_ref[PILLAR_PLACE[plane], inner, :])
+            same = table_ref[PILLAR_PLACE[plane], edge, :]
+            after = table_ref[PILLAR_PLACE[(plane + 1) % PLANE], edge, :]
+            parts.append(jnp.where(upper, after, same))
+        value = jnp.concatenate(parts, axis=0)
         top = value.astype(BF16).astype(F32)
         rest = pltpu.roll(value - top, LANES // 2, 1)
         columns.append(jnp.where(left, top, rest).astype(BF16))
@@ -319,12 +324,14 @@
 
 
 def select_kernel(mine_ref, table_ref, code_ref, sum_ref, send_ref):
-    coherence = jnp.concatenate(split_table(table_ref), axis=1)
+    coherence = jnp.concatenate(split_table(mine_ref, table_ref), axis=1)
     row = iota((2 * SPAN, LANES), 0) - SPAN * (mine_ref[0] % 2)
     extra = []
     for part in range(2):
         wanted = row == 4 * part + iota((2 * SPAN, LANES), 1) // OWN
-        extra.append(jnp.sum(jnp.where(wanted, sum_ref[...], 0.0), axis=0, keepdims=True))
+        extra.append(jnp.sum(jnp.where(wanted, sum_ref[0:2 * SPAN], 0.0), axis=0, keepdims=True))
+    wanted = row == iota((2 * SPAN, LANES), 1) // SPAN
+    extra.append(jnp.sum(jnp.where(wanted, sum_ref[2 * SPAN:], 0.0), axis=0, keepdims=True))
     extra = jnp.concatenate(extra, axis=0)
     step = 256
     half = iota((CAP // 2, LANES), 1) < LANES // 2
@@ -349,8 +356,8 @@
             send_ref[target + CAP // 2:target + ROWS, :] = extra
 
 
-def series_kernel(table_ref, high_ref, low_ref, series_ref):
-    columns = split_table(table_ref)
+def series_kernel(mine_ref, table_ref, high_ref, low_ref, series_ref):
+    columns = split_table(mine_ref, table_ref)
     series = jnp.zeros((DATES, LANES), F32)
     for lag in range(SPAN):
         rows = slice(lag * DATES, (lag + 1) * DATES)
@@ -376,6 +383,19 @@
                 moved = pltpu.roll(value, turn, 1) if turn else value
                 key = part, j, plane // 4
                 placed[key] = jnp.where(group == plane % 4, moved, placed[key]) if key in placed else moved
+    group = iota((PLANE, LANES), 1) // SPAN
+    sums = got_ref[pl.ds(CAP // 2 + 2, OWNERS, stride=ROWS), :] * (1.0 / 8192.0)
+    for plane in range(PLANE):
+        value = sums[plane * PLANE:(plane + 1) * PLANE]
+        value = value + pltpu.roll(value, 4, 0)
+        value = value + pltpu.roll(value, 2, 0)
+        target = (plane - 1) % PLANE
+        spot = (target % 4) * 4 + 3
+        for row in range(SPAN):
+            turn = SPAN * (spot - row) % LANES
+            moved = pltpu.roll(value, turn, 1) if turn else value
+            key = row // 4, row % 4, target // 4
+            placed[key] = placed[key] + jnp.where(group == spot, moved, 0.0)
     rows = [
         jnp.concatenate([placed[part, j, 0], placed[part, j, 1]], axis=1)[core:core + 1]
         for core in range(2) for part in range(2) for j in range(4)
@@ -510,14 +530,14 @@
     )(cells, table)
 
 
-def edge_coherence(cells, halo, table, inner, inner_sums):
+def edge_coherence(last, after, before, first, table, inner, inner_sums):
     return pl.pallas_call(
         edge_kernel,
         out_shape=(
             SHAPE((PLANE, SPAN // 2 * OWN, LANES), F32),
-            SHAPE((2 * SPAN, LANES), F32),
+            SHAPE((4 * SPAN, LANES), F32),
         ),
-        in_specs=vmem(5),
+        in_specs=vmem(7),
         out_specs=tuple(vmem(2)),
         scratch_shapes=[
             pltpu.VMEM((4 * TOGETHER, 2 * SPAN * 8, LANES), F32),
@@ -527,7 +547,7 @@
         compiler_params=params(),
         name="edge",
         cost_estimate=cost(2_000_000_000, 4_000_000),
-    )(cells, halo, table, inner, inner_sums)
+    )(last, after, before, first, table, inner, inner_sums)
 
 
 def select(mine, coherence, code, sums):
@@ -542,16 +562,16 @@
     )(mine, coherence, code, sums)
 
 
-def invert(coherence, high, low):
+def invert(mine, coherence, high, low):
     return pl.pallas_call(
         series_kernel,
         out_shape=SHAPE((2 * LOOKS, DATES), F32),
-        in_specs=vmem(3),
+        in_specs=SCALAR + vmem(3),
         out_specs=vmem(1)[0],
         compiler_params=params(WIDE_LIMIT),
         name="series",
         cost_estimate=cost(1_000_000_000, 3_000_000),
-    )(coherence, high, low)
+    )(mine, coherence, high, low)
 
 
 def output(got, high, low, own_early, own_lag, series):
@@ -574,16 +594,20 @@
     ordered = slot_order(mine, date_pairs, pair_owner, pseudo_inverse)
     cells, ordered = lax.optimization_barrier((cells, ordered))
     code, own_early, own_lag, high, low, table = ordered
-    first, last = (cells[PLANE_PLACE[w]:PLANE:PLANE // 2] for w in (0, PLANE - 2))
-    halo = lax.ppermute(first, "acq", [(i, (i - PLANE) % size) for i in range(size)])
+    first, last = (
+        [cells[PLANE_PLACE[w]:PLANE:PLANE // 2, half:half + HALF] for half in (0, HALF)]
+        for w in (0, PLANE - 2)
+    )
+    after = lax.ppermute(first[0], "acq", [(i, (i - PLANE) % size) for i in range(size)])
+    before = lax.ppermute(last[1], "acq", [(i, (i + PLANE) % size) for i in range(size)])
     inner, sums, table = inner_coherence(cells, table)
-    parts, sums = edge_coherence(last, halo, table, inner, sums)
+    parts, sums = edge_coherence(last[0], after, before, first[1], table, inner, sums)
     coherence = along(parts, pillars)
     packed = select(mine, coherence, code, exchange_sum(sums))
     got = lax.all_to_all(
         packed.reshape(OWNERS, 1, ROWS * LANES), "acq", split_axis=0, concat_axis=0, tiled=True
     ).reshape(OWNERS * ROWS, LANES)
-    series = invert(coherence, high, low)
+    series = invert(mine, coherence, high, low)
     series, slots = output(got, high, low, own_early, own_lag, series)
     return (
         series.reshape(1, 1, 2, LOOKS, DATES),

time: 106 us -> 102 us (0.962)
  waiting for transfers between devices: 51.5 us -> 47.2 us
    ppermute x1 -> x2, waiting for transfers between devices: 7.03 us -> 2.39 us  [the longest x1 2.38 us: on_device(): lax.ppermute(last[1], 'acq', [(i, (i + PLANE) % size) for i in range(size)])]
    ppermute x1 -> x2, starting transfers between devices: 4.86 us -> 4.95 us  [the longest x1 4.03 us: on_device(): lax.ppermute(first[0], 'acq', [(i, (i - PLANE) % size) for i in range(siz...]
  transfers between devices with their start and end apart: 8 -> 9, of which waited for: 7 -> 7; matrix products, arithmetic and copies ran while one was open for 0% -> 0% of each run, Pallas kernels for 11% -> 11%
where the time goes in v2:
time: 102 us
  waiting for transfers between devices  47.2 us (46%)
  starting transfers between devices  29.2 us (29%)
  Pallas kernels  21 us (21%)
  local copies, waits for them, and re-layouts  4.01 us (4%)
    all_to_all x2, waiting for transfers between devices, along(): lax.all_to_all(value, 'acq', split_axis=0, concat_axis=0, tiled=True, axi...  24 us
    all_to_all x1, waiting for transfers between devices, on_device(): lax.all_to_all(packed.reshape(OWNERS, 1, ROWS * LANES), 'acq', split_axis...  16.4 us
    all_to_all x2, starting transfers between devices, along(): lax.all_to_all(value, 'acq', split_axis=0, concat_axis=0, tiled=True, axi...  11.9 us
    all_to_all x1, starting transfers between devices, on_device(): lax.all_to_all(packed.reshape(OWNERS, 1, ROWS * LANES), 'acq', split_axis...  7.42 us
    ppermute x4, starting transfers between devices, exchange_sum(): lax.ppermute(value, axis, [(i, i ^ step) for i in range(size)])  5.01 us
    ppermute x4, waiting for transfers between devices, exchange_sum(): lax.ppermute(value, axis, [(i, i ^ step) for i in range(size)])  4.3 us
    pallas_call x1, Pallas kernels, slot_order(): pl.pallas_call(slot_kernel, out_shape=(SHAPE((16, SLOTS), F32), SHAPE((CA...  4.15 us
    ppermute x1, starting transfers between devices, on_device(): lax.ppermute(first[0], 'acq', [(i, (i - PLANE) % size) for i in range(siz...  4.03 us
  transfers between devices with their start and end apart: 9, of which 7 were waited for; matrix products, arithmetic and copies ran while one was open for 0% of the time, Pallas kernels for 11%

profile of v2, /device:TPU:1, one launch (start us, length us, event | category | flops | bytes accessed | tf_op | source)
XLA Modules:
  0.0 102.1 jit_solution(3364739495147359591)
XLA Ops:
  0.6 2.6 %pack.1 = bf16[8,8,128,128]{3,2,1,0:T(8,128)(2,1)} custom-call(bf16[8,64,2048]{2,1,0:T(8,128)(2,1)} %bitcast.11), custom_call_target="tpu_custom_call" | custom-call | tf_op jit(solution)/shard_map/pack/pallas_call | solution.py:476
  3.2 6.9 %all-to-all-start = ((bf16[8,8,128,128]{3,2,1,0:T(8,128)(2,1)}), bf16[8,8,128,128]{3,2,1,0:T(8,128)(2,1)S(1)}, u32[]{:S(2)}, u32[]{:S(2)}) async-start(bf16[8,8,128,128]{3,2,1,0:T(8,128)(2,1)} %pack.1), calls=%async_computation | async-start | bytes 4194304 | tf_op jit(solution)/shard_map/all_to_all | solution.py:454
  10.2 4.2 %slot_order.1 = (f32[16,2048]{1,0:T(8,128)S(1)}, f32[32,256]{1,0:T(8,128)S(1)}, f32[32,128]{1,0:T(8,128)S(1)}, bf16[256,2048]{1,0:T(8,128)(2,1)S(1)}, bf16[256,2...) custom-call(s32[1]{0:T(128)} %bitcast.mine_ref, s32[2,1024]{1,0:T(2,128)S(1)} %bitcast.9, s32[1,1024]{1,0:T(1,128)S(1)} %bitcast.10, ...), custom_call_target="tpu_custom_call" | custom-call | flops 4000000000 | bytes 8000000 | tf_op jit(solution)/shard_map/slot_order/pallas_call | solution.py:494
  14.3 1.0 copy-done
  15.3 1.0 copy-done.2
  16.3 1.1 %copy-done.9 = bf16[1024,640]{1,0:T(8,128)(2,1)} copy-done((bf16[1024,640]{1,0:T(8,128)(2,1)}, bf16[1024,640]{1,0:T(8,128)(2,1)S(1)}, u32[]{:S(2)}) %copy-start.9) | copy-done | bytes 1310744
  17.4 19.0 %all-to-all-done.cells_ref = bf16[8,8,128,128]{3,2,1,0:T(8,128)(2,1)S(1)} async-done(((bf16[8,8,128,128]{3,2,1,0:T(8,128)(2,1)}), bf16[8,8,128,128]{3,2,1,0:T(8,128)(2,1)S(1)}, u32[]{:S(2)}, u32[]{:S(2)}) %all-to-all-start) | async-done | bytes 2097184 | tf_op jit(solution)/shard_map/all_to_all | solution.py:454
  36.4 0.9 collective-permute-start.1
  37.4 4.0 %collective-permute-start = (bf16[2,4,128,128]{3,2,1,0:T(8,128)(2,1)S(1)}, bf16[2,4,128,128]{3,2,1,0:T(8,128)(2,1)S(1)}, u32[]{:S(2)}, u32[]{:S(2)}) collective-permute-start(bf16[2,4,128,128]{3,2,1,0:T(8,128)(2,1)S(1)} %get-tuple-element.48), channel_id=1, source_target_pairs={{0,224},{4,228},{8,232},{12,236},{16,240},{20,244},{24,248},{28,25... | collective-permute-start | bytes 786440 | tf_op jit(solution)/shard_map/ppermute | solution.py:601
  41.4 3.9 %coherence.1 = (f32[8,96,128]{2,1,0:T(8,128)S(1)}, f32[16,128]{1,0:T(8,128)S(1)}, bf16[1024,640]{1,0:T(8,128)(2,1)S(1)}) custom-call(bf16[8,8,128,128]{3,2,1,0:T(8,128)(2,1)S(1)} %all-to-all-done.cells_ref, bf16[1024,640]{1,0:T(8,128)(2,1)S(1)} %copy-done.10), custom_call_target="tpu_custom_call" | custom-call | flops 4000000000 | bytes 8000000 | tf_op jit(solution)/shard_map/coherence/pallas_call | solution.py:513
  45.3 2.4 %collective-permute-done.1.before_ref = bf16[2,4,128,128]{3,2,1,0:T(8,128)(2,1)S(1)} collective-permute-done((bf16[2,4,128,128]{3,2,1,0:T(8,128)(2,1)S(1)}, bf16[2,4,128,128]{3,2,1,0:T(8,128)(2,1)S(1)}, u32[]{:S(2)}, u32[]{:S(2)}) %collective-permute-start.1) | collective-permute-done | bytes 262176 | tf_op jit(solution)/shard_map/ppermute | solution.py:602
  47.7 2.7 %edge.1 = (f32[8,128,128]{2,1,0:T(8,128)}, f32[32,128]{1,0:T(8,128)S(1)}) custom-call(bf16[2,4,128,128]{3,2,1,0:T(8,128)(2,1)S(1)} %get-tuple-element.49.last_ref, bf16[2,4,128,128]{3,2,1,0:T(8,128)(2,1)S(1)} %collective-permute-done.next_ref, bf16[2,4,128,128]{3,2,1,0:T(8,128)(2,1)S(1)} %collective-permute-done.1.before_ref, ...), custom_call_target="tpu_custom_call" | custom-call | flops 2000000000 | bytes 4000000 | tf_op jit(solution)/shard_map/edge/pallas_call | solution.py:534
  50.4 5.0 %all-to-all-start.1 = ((f32[8,128,128]{2,1,0:T(8,128)}), f32[8,128,128]{2,1,0:T(8,128)S(1)}, u32[]{:S(2)}, u32[]{:S(2)}) async-start(f32[8,128,128]{2,1,0:T(8,128)} %get-tuple-element.33), calls=%async_computation.1 | async-start | bytes 1048576 | tf_op jit(solution)/shard_map/all_to_all | solution.py:454
  55.3 1.8 %collective-permute-start.2 = (f32[32,128]{1,0:T(8,128)S(1)}, f32[32,128]{1,0:T(8,128)S(1)}, u32[]{:S(2)}, u32[]{:S(2)}) collective-permute-start(f32[32,128]{1,0:T(8,128)S(1)} %get-tuple-element.35), channel_id=1, source_target_pairs={{0,4},{4,0},{8,12},{12,8},{16,20},{20,16},{24,28},{28,24},{32,36},... | collective-permute-start | bytes 49160 | tf_op jit(solution)/shard_map/ppermute | solution.py:463
  57.1 0.8 collective-permute-done.2
  57.9 2.5 %collective-permute-start.5 = (f32[32,128]{1,0:T(8,128)S(1)}, f32[32,128]{1,0:T(8,128)S(1)}, u32[]{:S(2)}, u32[]{:S(2)}) collective-permute-start(f32[32,128]{1,0:T(8,128)S(1)} %add.12), channel_id=1, source_target_pairs={{0,3},{1,2},{2,1},{3,0},{4,7},{5,6},{6,5},{7,4},{8,11},{9,10},{10,... | collective-permute-start | bytes 49160 | tf_op jit(solution)/shard_map/ppermute | solution.py:463
  61.7 2.9 %collective-permute-done.4 = f32[32,128]{1,0:T(8,128)S(1)} collective-permute-done((f32[32,128]{1,0:T(8,128)S(1)}, f32[32,128]{1,0:T(8,128)S(1)}, u32[]{:S(2)}, u32[]{:S(2)}) %collective-permute-start.4) | collective-permute-done | bytes 16416 | tf_op jit(solution)/shard_map/ppermute | solution.py:463
  64.7 5.1 %all-to-all-done.1.table_ref = f32[8,128,128]{2,1,0:T(8,128)S(1)} async-done(((f32[8,128,128]{2,1,0:T(8,128)}), f32[8,128,128]{2,1,0:T(8,128)S(1)}, u32[]{:S(2)}, u32[]{:S(2)}) %all-to-all-start.1) | async-done | bytes 524320 | tf_op jit(solution)/shard_map/all_to_all | solution.py:454
  69.7 2.4 %select.1 = f32[1216,128]{1,0:T(8,128)} custom-call(s32[1]{0:T(128)} %bitcast.mine_ref, f32[8,128,128]{2,1,0:T(8,128)S(1)} %all-to-all-done.1.table_ref, f32[16,2048]{1,0:T(8,128)S(1)} %get-tuple-element.34.code_ref, f32[32,128]{1,0:T(8,128)S(1)} %add_add_fusion.sum_ref), custom_call_target="tpu_custom_call" | custom-call | flops 2000000000 | bytes 4000000 | tf_op jit(solution)/shard_map/select/pallas_call | solution.py:554
  72.1 7.4 %all-to-all-start.2 = ((f32[64,1,2432]{2,1,0:T(1,128)}), f32[64,1,2432]{2,1,0:T(1,128)S(1)}, u32[]{:S(2)}, u32[]{:S(2)}) async-start(f32[64,1,2432]{2,1,0:T(1,128)} %bitcast.4), calls=%async_computation.2 | async-start | bytes 1245184 | tf_op jit(solution)/shard_map/all_to_all | solution.py:607
  79.6 3.4 %series.1.series_in_ref = f32[64,256]{1,0:T(8,128)} custom-call(s32[1]{0:T(128)} %bitcast.mine_ref, f32[8,128,128]{2,1,0:T(8,128)} %copy-done.4, bf16[256,2048]{1,0:T(8,128)(2,1)} %copy-done, bf16[256,2048]{1,0:T(8,128)(2,1)} %copy-done.2), custom_call_target="tpu_custom_call" | custom-call | flops 1000000000 | bytes 3000000 | tf_op jit(solution)/shard_map/series/pallas_call | solution.py:566
  83.0 16.4 %all-to-all-done.2 = f32[64,1,2432]{2,1,0:T(1,128)S(1)} async-done(((f32[64,1,2432]{2,1,0:T(1,128)}), f32[64,1,2432]{2,1,0:T(1,128)S(1)}, u32[]{:S(2)}, u32[]{:S(2)}) %all-to-all-start.2) | async-done | bytes 622624 | tf_op jit(solution)/shard_map/all_to_all | solution.py:607
  99.4 0.8 copy-done.5
  100.2 1.9 %referenced.1 = (f32[64,256]{1,0:T(8,128)}, f32[1024,128]{1,0:T(8,128)}) custom-call(f32[1216,128]{1,0:T(8,128)S(1)} %bitcast.8, bf16[256,2048]{1,0:T(8,128)(2,1)S(1)} %copy-done.1, bf16[256,2048]{1,0:T(8,128)(2,1)S(1)} %copy-done.3, f32[32,256]{1,0:T(8,128)S(1)} %get-tuple-element.38.own_early_ref, f32[32,128]{1,0:T(8,128)S(1)} %get-tuple-element.39.own_lag_ref, ...), custom_call_target="tpu_custom_call" | custom-call | tf_op jit(solution)/shard_map/referenced/pallas_call | solution.py:578
  (26 shorter events, 1.4 us)
Async XLA Ops:
  3.2 6.9 %copy-start.6 = (f32[256,1024]{1,0:T(8,128)S(1)}, f32[256,1024]{1,0:T(8,128)}, u32[]{:S(2)}) copy-start(f32[256,1024]{1,0:T(8,128)} %pinv_ref.1) | copy-start | bytes 3145732
  3.2 6.9 %copy-start.7 = (s32[1024,2]{0,1:T(2,128)S(1)}, s32[1024,2]{0,1:T(2,128)}, u32[]{:S(2)}) copy-start(s32[1024,2]{0,1:T(2,128)} %param.5) | copy-start | bytes 24580
  3.2 6.9 %copy-start.8 = (s32[1024,1]{0,1:T(1,128)S(1)}, s32[1024,1]{0,1:T(1,128)}, u32[]{:S(2)}) copy-start(s32[1024,1]{0,1:T(1,128)} %param.6) | copy-start | bytes 12292
  3.2 33.1 %all-to-all-start = ((bf16[8,8,128,128]{3,2,1,0:T(8,128)(2,1)}), bf16[8,8,128,128]{3,2,1,0:T(8,128)(2,1)S(1)}, u32[]{:S(2)}, u32[]{:S(2)}) async-start(bf16[8,8,128,128]{3,2,1,0:T(8,128)(2,1)} %pack.1), calls=%async_computation | async-start | bytes 4194304 | tf_op jit(solution)/shard_map/all_to_all | solution.py:454
  14.3 1.0 copy-start
  15.3 1.0 copy-start.2
  16.3 1.1 %copy-start.9 = (bf16[1024,640]{1,0:T(8,128)(2,1)}, bf16[1024,640]{1,0:T(8,128)(2,1)S(1)}, u32[]{:S(2)}) copy-start(bf16[1024,640]{1,0:T(8,128)(2,1)S(1)} %get-tuple-element.29.table_ref) | copy-start | bytes 3932164
  36.4 5.0 %copy-start.10 = (bf16[1024,640]{1,0:T(8,128)(2,1)S(1)}, bf16[1024,640]{1,0:T(8,128)(2,1)}, u32[]{:S(2)}) copy-start(bf16[1024,640]{1,0:T(8,128)(2,1)} %copy-done.9) | copy-start | bytes 3932164
  36.4 11.2 %collective-permute-start.1 = (bf16[2,4,128,128]{3,2,1,0:T(8,128)(2,1)S(1)}, bf16[2,4,128,128]{3,2,1,0:T(8,128)(2,1)S(1)}, u32[]{:S(2)}, u32[]{:S(2)}) collective-permute-start(bf16[2,4,128,128]{3,2,1,0:T(8,128)(2,1)S(1)} %get-tuple-element.47), channel_id=1, source_target_pairs={{0,32},{4,36},{8,40},{12,44},{16,48},{20,52},{24,56},{28,60},{32,6... | collective-permute-start | bytes 786440 | tf_op jit(solution)/shard_map/ppermute | solution.py:602
  37.4 10.3 %collective-permute-start = (bf16[2,4,128,128]{3,2,1,0:T(8,128)(2,1)S(1)}, bf16[2,4,128,128]{3,2,1,0:T(8,128)(2,1)S(1)}, u32[]{:S(2)}, u32[]{:S(2)}) collective-permute-start(bf16[2,4,128,128]{3,2,1,0:T(8,128)(2,1)S(1)} %get-tuple-element.48), channel_id=1, source_target_pairs={{0,224},{4,228},{8,232},{12,236},{16,240},{20,244},{24,248},{28,25... | collective-permute-start | bytes 786440 | tf_op jit(solution)/shard_map/ppermute | solution.py:601
  50.4 19.4 %all-to-all-start.1 = ((f32[8,128,128]{2,1,0:T(8,128)}), f32[8,128,128]{2,1,0:T(8,128)S(1)}, u32[]{:S(2)}, u32[]{:S(2)}) async-start(f32[8,128,128]{2,1,0:T(8,128)} %get-tuple-element.33), calls=%async_computation.1 | async-start | bytes 1048576 | tf_op jit(solution)/shard_map/all_to_all | solution.py:454
  55.3 2.6 %collective-permute-start.2 = (f32[32,128]{1,0:T(8,128)S(1)}, f32[32,128]{1,0:T(8,128)S(1)}, u32[]{:S(2)}, u32[]{:S(2)}) collective-permute-start(f32[32,128]{1,0:T(8,128)S(1)} %get-tuple-element.35), channel_id=1, source_target_pairs={{0,4},{4,0},{8,12},{12,8},{16,20},{20,16},{24,28},{28,24},{32,36},... | collective-permute-start | bytes 49160 | tf_op jit(solution)/shard_map/ppermute | solution.py:463
  57.9 3.8 %collective-permute-start.5 = (f32[32,128]{1,0:T(8,128)S(1)}, f32[32,128]{1,0:T(8,128)S(1)}, u32[]{:S(2)}, u32[]{:S(2)}) collective-permute-start(f32[32,128]{1,0:T(8,128)S(1)} %add.12), channel_id=1, source_target_pairs={{0,3},{1,2},{2,1},{3,0},{4,7},{5,6},{6,5},{7,4},{8,11},{9,10},{10,... | collective-permute-start | bytes 49160 | tf_op jit(solution)/shard_map/ppermute | solution.py:463
  60.4 4.2 %collective-permute-start.4 = (f32[32,128]{1,0:T(8,128)S(1)}, f32[32,128]{1,0:T(8,128)S(1)}, u32[]{:S(2)}, u32[]{:S(2)}) collective-permute-start(f32[32,128]{1,0:T(8,128)S(1)} %add.12), channel_id=1, source_target_pairs={{0,2},{1,3},{2,0},{3,1},{4,6},{5,7},{6,4},{7,5},{8,10},{9,11},{10,... | collective-permute-start | bytes 49160 | tf_op jit(solution)/shard_map/ppermute | solution.py:463
  60.9 3.7 %collective-permute-start.3 = (f32[32,128]{1,0:T(8,128)S(1)}, f32[32,128]{1,0:T(8,128)S(1)}, u32[]{:S(2)}, u32[]{:S(2)}) collective-permute-start(f32[32,128]{1,0:T(8,128)S(1)} %add.12), channel_id=1, source_target_pairs={{0,1},{1,0},{2,3},{3,2},{4,5},{5,4},{6,7},{7,6},{8,9},{9,8},{10,11... | collective-permute-start | bytes 49160 | tf_op jit(solution)/shard_map/ppermute | solution.py:463
  69.7 2.4 %copy-start.4 = (f32[8,128,128]{2,1,0:T(8,128)}, f32[8,128,128]{2,1,0:T(8,128)S(1)}, u32[]{:S(2)}) copy-start(f32[8,128,128]{2,1,0:T(8,128)S(1)} %all-to-all-done.1.table_ref) | copy-start | bytes 1572868
  72.1 27.3 %all-to-all-start.2 = ((f32[64,1,2432]{2,1,0:T(1,128)}), f32[64,1,2432]{2,1,0:T(1,128)S(1)}, u32[]{:S(2)}, u32[]{:S(2)}) async-start(f32[64,1,2432]{2,1,0:T(1,128)} %bitcast.4), calls=%async_computation.2 | async-start | bytes 1245184 | tf_op jit(solution)/shard_map/all_to_all | solution.py:607
  79.6 19.8 %copy-start.1 = (bf16[256,2048]{1,0:T(8,128)(2,1)S(1)}, bf16[256,2048]{1,0:T(8,128)(2,1)}, u32[]{:S(2)}) copy-start(bf16[256,2048]{1,0:T(8,128)(2,1)} %copy-done) | copy-start | bytes 3145732
  79.6 19.8 %copy-start.3 = (bf16[256,2048]{1,0:T(8,128)(2,1)S(1)}, bf16[256,2048]{1,0:T(8,128)(2,1)}, u32[]{:S(2)}) copy-start(bf16[256,2048]{1,0:T(8,128)(2,1)} %copy-done.2) | copy-start | bytes 3145732
  99.4 0.8 copy-start.5

commit v3 on v2

--- a/solution.py
+++ b/solution.py
@@ -23,8 +23,12 @@
 HALF = PLANE // 2
 PLANE_ORDER = (0, 2, 4, 6, 1, 3, 5, 7)
 PLANE_PLACE = tuple(PLANE_ORDER.index(w) for w in range(PLANE))
-PILLAR_ORDER = (0, 3, 6, 1, 4, 7, 2, 5)
+PILLAR_ORDER = (0, 4, 1, 5, 2, 6, 3, 7)
 PILLAR_PLACE = tuple(PILLAR_ORDER.index(z) for z in range(PLANE))
+SLOT_ORDER = (0, 4, 1, 5, 2, 6, 3, 7)
+SLOT_PLACE = tuple(
+    SLOT_ORDER.index(owner // PLANE) * PLANE + owner % PLANE for owner in range(OWNERS)
+)
 TABLE = (1 + SPAN // 2) * LANES
 VMEM_LIMIT = 20 * 1024 * 1024
 WIDE_LIMIT = 58 * 1024 * 1024
@@ -349,7 +353,7 @@
         for part in range(step // CAP):
             first = part * CAP
             middle = first + CAP // 2
-            target = (start // CAP + part) * ROWS
+            target = SLOT_PLACE[start // CAP + part] * ROWS
             send_ref[target:target + CAP // 2, :] = jnp.where(
                 half, value[first:middle], value[middle:first + CAP]
             )
@@ -375,7 +379,8 @@
     for part in range(2):
         sums = got_ref[pl.ds(CAP // 2 + part, OWNERS, stride=ROWS), :] * (1.0 / 8192.0)
         for plane in range(PLANE):
-            value = sums[plane * PLANE:(plane + 1) * PLANE]
+            start = SLOT_PLACE[plane * PLANE]
+            value = sums[start:start + PLANE]
             value = value + pltpu.roll(value, 4, 0)
             value = value + pltpu.roll(value, 2, 0)
             for j in range(4):
@@ -386,7 +391,8 @@
     group = iota((PLANE, LANES), 1) // SPAN
     sums = got_ref[pl.ds(CAP // 2 + 2, OWNERS, stride=ROWS), :] * (1.0 / 8192.0)
     for plane in range(PLANE):
-        value = sums[plane * PLANE:(plane + 1) * PLANE]
+        start = SLOT_PLACE[plane * PLANE]
+        value = sums[start:start + PLANE]
         value = value + pltpu.roll(value, 4, 0)
         value = value + pltpu.roll(value, 2, 0)
         target = (plane - 1) % PLANE
@@ -423,9 +429,8 @@
         means.append(jnp.sum(found[kind] * own_early_ref[...], axis=1, keepdims=True))
     chunk = iota((CAP // 2, LANES), 1) // LOOKS
     for block in range(OWNERS // 4):
-        parts = [
-            got_ref[(4 * block + j) * ROWS:(4 * block + j) * ROWS + CAP // 2, :] for j in range(4)
-        ]
+        starts = [SLOT_PLACE[4 * block + j] * ROWS for j in range(4)]
+        parts = [got_ref[start:start + CAP // 2, :] for start in starts]
         for t in range(4):
             side, kind = t // 2, t % 2
             result = None
@@ -604,9 +609,8 @@
     parts, sums = edge_coherence(last[0], after, before, first[1], table, inner, sums)
     coherence = along(parts, pillars)
     packed = select(mine, coherence, code, exchange_sum(sums))
-    got = lax.all_to_all(
-        packed.reshape(OWNERS, 1, ROWS * LANES), "acq", split_axis=0, concat_axis=0, tiled=True
-    ).reshape(OWNERS * ROWS, LANES)
+    everyone = [[PLANE * z + w for z in SLOT_ORDER for w in range(PLANE)]]
+    got = along(packed.reshape(OWNERS, 1, ROWS * LANES), everyone).reshape(OWNERS * ROWS, LANES)
     series = invert(mine, coherence, high, low)
     series, slots = output(got, high, low, own_early, own_lag, series)
     return (

time: 102 us -> 102 us (level)
  waiting for transfers between devices: 47.2 us -> 45.7 us
    all_to_all x1 -> x0, waiting for transfers between devices: 16.4 us -> none  [on_device(): lax.all_to_all(packed.reshape(OWNERS, 1, ROWS * LANES), 'acq', split_axis...]
    all_to_all x2 -> x3, waiting for transfers between devices: 24 us -> 39 us  [along(): lax.all_to_all(value, 'acq', split_axis=0, concat_axis=0, tiled=True, axi...]
    all_to_all x2 -> x3, starting transfers between devices: 11.9 us -> 20.2 us  [along(): lax.all_to_all(value, 'acq', split_axis=0, concat_axis=0, tiled=True, axi...]
    all_to_all x1 -> x0, starting transfers between devices: 7.42 us -> none  [on_device(): lax.all_to_all(packed.reshape(OWNERS, 1, ROWS * LANES), 'acq', split_axis...]
where the time goes in v3:
time: 102 us
  waiting for transfers between devices  45.7 us (45%)
  starting transfers between devices  30.1 us (30%)
  Pallas kernels  20.9 us (20%)
  local copies, waits for them, and re-layouts  4.01 us (4%)
    all_to_all x3, waiting for transfers between devices, along(): lax.all_to_all(value, 'acq', split_axis=0, concat_axis=0, tiled=True, axi...  39 us
    all_to_all x3, starting transfers between devices, along(): lax.all_to_all(value, 'acq', split_axis=0, concat_axis=0, tiled=True, axi...  20.2 us
    ppermute x4, starting transfers between devices, exchange_sum(): lax.ppermute(value, axis, [(i, i ^ step) for i in range(size)])  5.01 us
    ppermute x4, waiting for transfers between devices, exchange_sum(): lax.ppermute(value, axis, [(i, i ^ step) for i in range(size)])  4.3 us
    pallas_call x1, Pallas kernels, slot_order(): pl.pallas_call(slot_kernel, out_shape=(SHAPE((16, SLOTS), F32), SHAPE((CA...  4.15 us
    ppermute x1, starting transfers between devices, on_device(): lax.ppermute(first[0], 'acq', [(i, (i - PLANE) % size) for i in range(siz...  4.03 us
    unnamed x22, local copies, waits for them, and re-layouts  3.94 us
    pallas_call x1, Pallas kernels, inner_coherence(): pl.pallas_call(inner_kernel, out_shape=(SHAPE((PLANE, SPAN // 2 * INNER,...  3.91 us
  transfers between devices with their start and end apart: 9, of which 7 were waited for; matrix products, arithmetic and copies ran while one was open for 0% of the time, Pallas kernels for 11%

profile of v3, /device:TPU:1, one launch (start us, length us, event | category | flops | bytes accessed | tf_op | source)
XLA Modules:
  0.0 101.5 jit_solution(4269375420311575709)
XLA Ops:
  0.6 2.6 %pack.1 = bf16[8,8,128,128]{3,2,1,0:T(8,128)(2,1)} custom-call(bf16[8,64,2048]{2,1,0:T(8,128)(2,1)} %bitcast.11), custom_call_target="tpu_custom_call" | custom-call | tf_op jit(solution)/shard_map/pack/pallas_call | solution.py:481
  3.2 6.9 %all-to-all-start = ((bf16[8,8,128,128]{3,2,1,0:T(8,128)(2,1)}), bf16[8,8,128,128]{3,2,1,0:T(8,128)(2,1)S(1)}, u32[]{:S(2)}, u32[]{:S(2)}) async-start(bf16[8,8,128,128]{3,2,1,0:T(8,128)(2,1)} %pack.1), calls=%async_computation | async-start | bytes 4194304 | tf_op jit(solution)/shard_map/all_to_all | solution.py:459
  10.2 4.2 %slot_order.1 = (f32[16,2048]{1,0:T(8,128)S(1)}, f32[32,256]{1,0:T(8,128)S(1)}, f32[32,128]{1,0:T(8,128)S(1)}, bf16[256,2048]{1,0:T(8,128)(2,1)S(1)}, bf16[256,2...) custom-call(s32[1]{0:T(128)} %bitcast.mine_ref, s32[2,1024]{1,0:T(2,128)S(1)} %bitcast.9, s32[1,1024]{1,0:T(1,128)S(1)} %bitcast.10, ...), custom_call_target="tpu_custom_call" | custom-call | flops 4000000000 | bytes 8000000 | tf_op jit(solution)/shard_map/slot_order/pallas_call | solution.py:499
  14.3 1.0 copy-done
  15.3 1.0 copy-done.2
  16.3 1.1 %copy-done.9 = bf16[1024,640]{1,0:T(8,128)(2,1)} copy-done((bf16[1024,640]{1,0:T(8,128)(2,1)}, bf16[1024,640]{1,0:T(8,128)(2,1)S(1)}, u32[]{:S(2)}) %copy-start.9) | copy-done | bytes 1310744
  17.4 19.0 %all-to-all-done.cells_ref = bf16[8,8,128,128]{3,2,1,0:T(8,128)(2,1)S(1)} async-done(((bf16[8,8,128,128]{3,2,1,0:T(8,128)(2,1)}), bf16[8,8,128,128]{3,2,1,0:T(8,128)(2,1)S(1)}, u32[]{:S(2)}, u32[]{:S(2)}) %all-to-all-start) | async-done | bytes 2097184 | tf_op jit(solution)/shard_map/all_to_all | solution.py:459
  36.4 0.9 collective-permute-start.1
  37.4 4.0 %collective-permute-start = (bf16[2,4,128,128]{3,2,1,0:T(8,128)(2,1)S(1)}, bf16[2,4,128,128]{3,2,1,0:T(8,128)(2,1)S(1)}, u32[]{:S(2)}, u32[]{:S(2)}) collective-permute-start(bf16[2,4,128,128]{3,2,1,0:T(8,128)(2,1)S(1)} %get-tuple-element.48), channel_id=1, source_target_pairs={{0,224},{4,228},{8,232},{12,236},{16,240},{20,244},{24,248},{28,25... | collective-permute-start | bytes 786440 | tf_op jit(solution)/shard_map/ppermute | solution.py:606
  41.4 3.9 %coherence.1 = (f32[8,96,128]{2,1,0:T(8,128)S(1)}, f32[16,128]{1,0:T(8,128)S(1)}, bf16[1024,640]{1,0:T(8,128)(2,1)S(1)}) custom-call(bf16[8,8,128,128]{3,2,1,0:T(8,128)(2,1)S(1)} %all-to-all-done.cells_ref, bf16[1024,640]{1,0:T(8,128)(2,1)S(1)} %copy-done.10), custom_call_target="tpu_custom_call" | custom-call | flops 4000000000 | bytes 8000000 | tf_op jit(solution)/shard_map/coherence/pallas_call | solution.py:518
  45.3 2.4 %collective-permute-done.1.before_ref = bf16[2,4,128,128]{3,2,1,0:T(8,128)(2,1)S(1)} collective-permute-done((bf16[2,4,128,128]{3,2,1,0:T(8,128)(2,1)S(1)}, bf16[2,4,128,128]{3,2,1,0:T(8,128)(2,1)S(1)}, u32[]{:S(2)}, u32[]{:S(2)}) %collective-permute-start.1) | collective-permute-done | bytes 262176 | tf_op jit(solution)/shard_map/ppermute | solution.py:607
  47.7 2.7 %edge.1 = (f32[8,128,128]{2,1,0:T(8,128)}, f32[32,128]{1,0:T(8,128)S(1)}) custom-call(bf16[2,4,128,128]{3,2,1,0:T(8,128)(2,1)S(1)} %get-tuple-element.49.last_ref, bf16[2,4,128,128]{3,2,1,0:T(8,128)(2,1)S(1)} %collective-permute-done.next_ref, bf16[2,4,128,128]{3,2,1,0:T(8,128)(2,1)S(1)} %collective-permute-done.1.before_ref, ...), custom_call_target="tpu_custom_call" | custom-call | flops 2000000000 | bytes 4000000 | tf_op jit(solution)/shard_map/edge/pallas_call | solution.py:539
  50.4 5.0 %all-to-all-start.1 = ((f32[8,128,128]{2,1,0:T(8,128)}), f32[8,128,128]{2,1,0:T(8,128)S(1)}, u32[]{:S(2)}, u32[]{:S(2)}) async-start(f32[8,128,128]{2,1,0:T(8,128)} %get-tuple-element.33), calls=%async_computation.1 | async-start | bytes 1048576 | tf_op jit(solution)/shard_map/all_to_all | solution.py:459
  55.3 1.8 %collective-permute-start.2 = (f32[32,128]{1,0:T(8,128)S(1)}, f32[32,128]{1,0:T(8,128)S(1)}, u32[]{:S(2)}, u32[]{:S(2)}) collective-permute-start(f32[32,128]{1,0:T(8,128)S(1)} %get-tuple-element.35), channel_id=1, source_target_pairs={{0,4},{4,0},{8,12},{12,8},{16,20},{20,16},{24,28},{28,24},{32,36},... | collective-permute-start | bytes 49160 | tf_op jit(solution)/shard_map/ppermute | solution.py:468
  57.1 0.8 collective-permute-done.2
  57.9 2.5 %collective-permute-start.5 = (f32[32,128]{1,0:T(8,128)S(1)}, f32[32,128]{1,0:T(8,128)S(1)}, u32[]{:S(2)}, u32[]{:S(2)}) collective-permute-start(f32[32,128]{1,0:T(8,128)S(1)} %add.12), channel_id=1, source_target_pairs={{0,3},{1,2},{2,1},{3,0},{4,7},{5,6},{6,5},{7,4},{8,11},{9,10},{10,... | collective-permute-start | bytes 49160 | tf_op jit(solution)/shard_map/ppermute | solution.py:468
  61.7 2.9 %collective-permute-done.4 = f32[32,128]{1,0:T(8,128)S(1)} collective-permute-done((f32[32,128]{1,0:T(8,128)S(1)}, f32[32,128]{1,0:T(8,128)S(1)}, u32[]{:S(2)}, u32[]{:S(2)}) %collective-permute-start.4) | collective-permute-done | bytes 16416 | tf_op jit(solution)/shard_map/ppermute | solution.py:468
  64.7 3.7 %all-to-all-done.1.table_ref = f32[8,128,128]{2,1,0:T(8,128)S(1)} async-done(((f32[8,128,128]{2,1,0:T(8,128)}), f32[8,128,128]{2,1,0:T(8,128)S(1)}, u32[]{:S(2)}, u32[]{:S(2)}) %all-to-all-start.1) | async-done | bytes 524320 | tf_op jit(solution)/shard_map/all_to_all | solution.py:459
  68.4 2.4 %select.1 = f32[1216,128]{1,0:T(8,128)} custom-call(s32[1]{0:T(128)} %bitcast.mine_ref, f32[8,128,128]{2,1,0:T(8,128)S(1)} %all-to-all-done.1.table_ref, f32[16,2048]{1,0:T(8,128)S(1)} %get-tuple-element.34.code_ref, f32[32,128]{1,0:T(8,128)S(1)} %add_add_fusion.sum_ref), custom_call_target="tpu_custom_call" | custom-call | flops 2000000000 | bytes 4000000 | tf_op jit(solution)/shard_map/select/pallas_call | solution.py:559
  70.8 8.3 %all-to-all-start.2 = ((f32[64,1,2432]{2,1,0:T(1,128)}), f32[64,1,2432]{2,1,0:T(1,128)S(1)}, u32[]{:S(2)}, u32[]{:S(2)}) async-start(f32[64,1,2432]{2,1,0:T(1,128)} %bitcast.4), calls=%async_computation.2 | async-start | bytes 1245184 | tf_op jit(solution)/shard_map/all_to_all | solution.py:459
  79.1 3.4 %series.1.series_in_ref = f32[64,256]{1,0:T(8,128)} custom-call(s32[1]{0:T(128)} %bitcast.mine_ref, f32[8,128,128]{2,1,0:T(8,128)} %copy-done.4, bf16[256,2048]{1,0:T(8,128)(2,1)} %copy-done, bf16[256,2048]{1,0:T(8,128)(2,1)} %copy-done.2), custom_call_target="tpu_custom_call" | custom-call | flops 1000000000 | bytes 3000000 | tf_op jit(solution)/shard_map/series/pallas_call | solution.py:571
  82.5 16.3 %all-to-all-done.2 = f32[64,1,2432]{2,1,0:T(1,128)S(1)} async-done(((f32[64,1,2432]{2,1,0:T(1,128)}), f32[64,1,2432]{2,1,0:T(1,128)S(1)}, u32[]{:S(2)}, u32[]{:S(2)}) %all-to-all-start.2) | async-done | bytes 622624 | tf_op jit(solution)/shard_map/all_to_all | solution.py:459
  98.8 0.8 copy-done.5
  99.6 1.9 %referenced.1 = (f32[64,256]{1,0:T(8,128)}, f32[1024,128]{1,0:T(8,128)}) custom-call(f32[1216,128]{1,0:T(8,128)S(1)} %bitcast.8, bf16[256,2048]{1,0:T(8,128)(2,1)S(1)} %copy-done.1, bf16[256,2048]{1,0:T(8,128)(2,1)S(1)} %copy-done.3, f32[32,256]{1,0:T(8,128)S(1)} %get-tuple-element.38.own_early_ref, f32[32,128]{1,0:T(8,128)S(1)} %get-tuple-element.39.own_lag_ref, ...), custom_call_target="tpu_custom_call" | custom-call | tf_op jit(solution)/shard_map/referenced/pallas_call | solution.py:583
  (26 shorter events, 1.4 us)
Async XLA Ops:
  3.2 6.9 %copy-start.6 = (f32[256,1024]{1,0:T(8,128)S(1)}, f32[256,1024]{1,0:T(8,128)}, u32[]{:S(2)}) copy-start(f32[256,1024]{1,0:T(8,128)} %pinv_ref.1) | copy-start | bytes 3145732
  3.2 6.9 %copy-start.7 = (s32[1024,2]{0,1:T(2,128)S(1)}, s32[1024,2]{0,1:T(2,128)}, u32[]{:S(2)}) copy-start(s32[1024,2]{0,1:T(2,128)} %param.5) | copy-start | bytes 24580
  3.2 6.9 %copy-start.8 = (s32[1024,1]{0,1:T(1,128)S(1)}, s32[1024,1]{0,1:T(1,128)}, u32[]{:S(2)}) copy-start(s32[1024,1]{0,1:T(1,128)} %param.6) | copy-start | bytes 12292
  3.2 33.1 %all-to-all-start = ((bf16[8,8,128,128]{3,2,1,0:T(8,128)(2,1)}), bf16[8,8,128,128]{3,2,1,0:T(8,128)(2,1)S(1)}, u32[]{:S(2)}, u32[]{:S(2)}) async-start(bf16[8,8,128,128]{3,2,1,0:T(8,128)(2,1)} %pack.1), calls=%async_computation | async-start | bytes 4194304 | tf_op jit(solution)/shard_map/all_to_all | solution.py:459
  14.3 1.0 copy-start
  15.3 1.0 copy-start.2
  16.3 1.1 %copy-start.9 = (bf16[1024,640]{1,0:T(8,128)(2,1)}, bf16[1024,640]{1,0:T(8,128)(2,1)S(1)}, u32[]{:S(2)}) copy-start(bf16[1024,640]{1,0:T(8,128)(2,1)S(1)} %get-tuple-element.29.table_ref) | copy-start | bytes 3932164
  36.4 5.0 %copy-start.10 = (bf16[1024,640]{1,0:T(8,128)(2,1)S(1)}, bf16[1024,640]{1,0:T(8,128)(2,1)}, u32[]{:S(2)}) copy-start(bf16[1024,640]{1,0:T(8,128)(2,1)} %copy-done.9) | copy-start | bytes 3932164
  36.4 11.2 %collective-permute-start.1 = (bf16[2,4,128,128]{3,2,1,0:T(8,128)(2,1)S(1)}, bf16[2,4,128,128]{3,2,1,0:T(8,128)(2,1)S(1)}, u32[]{:S(2)}, u32[]{:S(2)}) collective-permute-start(bf16[2,4,128,128]{3,2,1,0:T(8,128)(2,1)S(1)} %get-tuple-element.47), channel_id=1, source_target_pairs={{0,32},{4,36},{8,40},{12,44},{16,48},{20,52},{24,56},{28,60},{32,6... | collective-permute-start | bytes 786440 | tf_op jit(solution)/shard_map/ppermute | solution.py:607
  37.4 10.3 %collective-permute-start = (bf16[2,4,128,128]{3,2,1,0:T(8,128)(2,1)S(1)}, bf16[2,4,128,128]{3,2,1,0:T(8,128)(2,1)S(1)}, u32[]{:S(2)}, u32[]{:S(2)}) collective-permute-start(bf16[2,4,128,128]{3,2,1,0:T(8,128)(2,1)S(1)} %get-tuple-element.48), channel_id=1, source_target_pairs={{0,224},{4,228},{8,232},{12,236},{16,240},{20,244},{24,248},{28,25... | collective-permute-start | bytes 786440 | tf_op jit(solution)/shard_map/ppermute | solution.py:606
  50.4 18.0 %all-to-all-start.1 = ((f32[8,128,128]{2,1,0:T(8,128)}), f32[8,128,128]{2,1,0:T(8,128)S(1)}, u32[]{:S(2)}, u32[]{:S(2)}) async-start(f32[8,128,128]{2,1,0:T(8,128)} %get-tuple-element.33), calls=%async_computation.1 | async-start | bytes 1048576 | tf_op jit(solution)/shard_map/all_to_all | solution.py:459
  55.3 2.6 %collective-permute-start.2 = (f32[32,128]{1,0:T(8,128)S(1)}, f32[32,128]{1,0:T(8,128)S(1)}, u32[]{:S(2)}, u32[]{:S(2)}) collective-permute-start(f32[32,128]{1,0:T(8,128)S(1)} %get-tuple-element.35), channel_id=1, source_target_pairs={{0,4},{4,0},{8,12},{12,8},{16,20},{20,16},{24,28},{28,24},{32,36},... | collective-permute-start | bytes 49160 | tf_op jit(solution)/shard_map/ppermute | solution.py:468
  57.9 3.8 %collective-permute-start.5 = (f32[32,128]{1,0:T(8,128)S(1)}, f32[32,128]{1,0:T(8,128)S(1)}, u32[]{:S(2)}, u32[]{:S(2)}) collective-permute-start(f32[32,128]{1,0:T(8,128)S(1)} %add.12), channel_id=1, source_target_pairs={{0,3},{1,2},{2,1},{3,0},{4,7},{5,6},{6,5},{7,4},{8,11},{9,10},{10,... | collective-permute-start | bytes 49160 | tf_op jit(solution)/shard_map/ppermute | solution.py:468
  60.4 4.2 %collective-permute-start.4 = (f32[32,128]{1,0:T(8,128)S(1)}, f32[32,128]{1,0:T(8,128)S(1)}, u32[]{:S(2)}, u32[]{:S(2)}) collective-permute-start(f32[32,128]{1,0:T(8,128)S(1)} %add.12), channel_id=1, source_target_pairs={{0,2},{1,3},{2,0},{3,1},{4,6},{5,7},{6,4},{7,5},{8,10},{9,11},{10,... | collective-permute-start | bytes 49160 | tf_op jit(solution)/shard_map/ppermute | solution.py:468
  60.9 3.7 %collective-permute-start.3 = (f32[32,128]{1,0:T(8,128)S(1)}, f32[32,128]{1,0:T(8,128)S(1)}, u32[]{:S(2)}, u32[]{:S(2)}) collective-permute-start(f32[32,128]{1,0:T(8,128)S(1)} %add.12), channel_id=1, source_target_pairs={{0,1},{1,0},{2,3},{3,2},{4,5},{5,4},{6,7},{7,6},{8,9},{9,8},{10,11... | collective-permute-start | bytes 49160 | tf_op jit(solution)/shard_map/ppermute | solution.py:468
  68.4 2.4 %copy-start.4 = (f32[8,128,128]{2,1,0:T(8,128)}, f32[8,128,128]{2,1,0:T(8,128)S(1)}, u32[]{:S(2)}) copy-start(f32[8,128,128]{2,1,0:T(8,128)S(1)} %all-to-all-done.1.table_ref) | copy-start | bytes 1572868
  70.8 28.0 %all-to-all-start.2 = ((f32[64,1,2432]{2,1,0:T(1,128)}), f32[64,1,2432]{2,1,0:T(1,128)S(1)}, u32[]{:S(2)}, u32[]{:S(2)}) async-start(f32[64,1,2432]{2,1,0:T(1,128)} %bitcast.4), calls=%async_computation.2 | async-start | bytes 1245184 | tf_op jit(solution)/shard_map/all_to_all | solution.py:459
  79.1 19.7 %copy-start.1 = (bf16[256,2048]{1,0:T(8,128)(2,1)S(1)}, bf16[256,2048]{1,0:T(8,128)(2,1)}, u32[]{:S(2)}) copy-start(bf16[256,2048]{1,0:T(8,128)(2,1)} %copy-done) | copy-start | bytes 3145732
  79.1 19.7 %copy-start.3 = (bf16[256,2048]{1,0:T(8,128)(2,1)S(1)}, bf16[256,2048]{1,0:T(8,128)(2,1)}, u32[]{:S(2)}) copy-start(bf16[256,2048]{1,0:T(8,128)(2,1)} %copy-done.2) | copy-start | bytes 3145732
  98.8 0.8 copy-start.5

commit v4 on v3

--- a/solution.py
+++ b/solution.py
@@ -30,7 +30,7 @@
     SLOT_ORDER.index(owner // PLANE) * PLANE + owner % PLANE for owner in range(OWNERS)
 )
 TABLE = (1 + SPAN // 2) * LANES
-VMEM_LIMIT = 20 * 1024 * 1024
+VMEM_LIMIT = 50 * 1024 * 1024
 WIDE_LIMIT = 58 * 1024 * 1024
 F32 = jnp.float32
 BF16 = jnp.bfloat16

time: 102 us -> 103 us (level)
  Pallas kernels: 20.9 us -> 22.5 us
    ppermute x1, waiting for transfers between devices: 2.38 us -> 0.79 us  [on_device(): lax.ppermute(last[1], 'acq', [(i, (i + PLANE) % size) for i in range(size)])]
    pallas_call x1, Pallas kernels: 3.91 us -> 5.51 us  [inner_coherence(): pl.pallas_call(inner_kernel, out_shape=(SHAPE((PLANE, SPAN // 2 * INNER,...]
    all_to_all x3, waiting for transfers between devices: 39 us -> 40.2 us  [along(): lax.all_to_all(value, 'acq', split_axis=0, concat_axis=0, tiled=True, axi...]
    slice x1, local copies, waits for them, and re-layouts: 0.07 us -> 1.27 us  [on_device(): cells[PLANE_PLACE[w]:PLANE:PLANE // 2, half:half + HALF]]
    unnamed x22 -> x20, local copies, waits for them, and re-layouts: 3.94 us -> 2.84 us
  transfers between devices with their start and end apart: 9 -> 9, of which waited for: 7 -> 7; matrix products, arithmetic and copies ran while one was open for 0% -> 0% of each run, Pallas kernels for 11% -> 13%
where the time goes in v4:
time: 103 us
  waiting for transfers between devices  45.3 us (44%)
  starting transfers between devices  30.1 us (29%)
  Pallas kernels  22.5 us (22%)
  local copies, waits for them, and re-layouts  4.11 us (4%)
    all_to_all x3, waiting for transfers between devices, along(): lax.all_to_all(value, 'acq', split_axis=0, concat_axis=0, tiled=True, axi...  40.2 us
    all_to_all x3, starting transfers between devices, along(): lax.all_to_all(value, 'acq', split_axis=0, concat_axis=0, tiled=True, axi...  20.9 us
    pallas_call x1, Pallas kernels, inner_coherence(): pl.pallas_call(inner_kernel, out_shape=(SHAPE((PLANE, SPAN // 2 * INNER,...  5.51 us
    ppermute x4, starting transfers between devices, exchange_sum(): lax.ppermute(value, axis, [(i, i ^ step) for i in range(size)])  5 us
    ppermute x4, waiting for transfers between devices, exchange_sum(): lax.ppermute(value, axis, [(i, i ^ step) for i in range(size)])  4.29 us
    pallas_call x1, Pallas kernels, slot_order(): pl.pallas_call(slot_kernel, out_shape=(SHAPE((16, SLOTS), F32), SHAPE((CA...  4.16 us
    ppermute x1, starting transfers between devices, on_device(): lax.ppermute(first[0], 'acq', [(i, (i - PLANE) % size) for i in range(siz...  4.03 us
    pallas_call x1, Pallas kernels, invert(): pl.pallas_call(series_kernel, out_shape=SHAPE((2 * LOOKS, DATES), F32), i...  3.38 us
  transfers between devices with their start and end apart: 9, of which 7 were waited for; matrix products, arithmetic and copies ran while one was open for 0% of the time, Pallas kernels for 13%

profile of v4, /device:TPU:1, one launch (start us, length us, event | category | flops | bytes accessed | tf_op | source)
XLA Modules:
  0.0 102.8 jit_solution(6465034295473715171)
XLA Ops:
  0.6 2.5 %pack.1 = bf16[8,8,128,128]{3,2,1,0:T(8,128)(2,1)} custom-call(bf16[8,64,2048]{2,1,0:T(8,128)(2,1)} %bitcast.11), custom_call_target="tpu_custom_call" | custom-call | tf_op jit(solution)/shard_map/pack/pallas_call | solution.py:481
  3.2 7.6 %all-to-all-start = ((bf16[8,8,128,128]{3,2,1,0:T(8,128)(2,1)}), bf16[8,8,128,128]{3,2,1,0:T(8,128)(2,1)}, u32[]{:S(2)}, u32[]{:S(2)}) async-start(bf16[8,8,128,128]{3,2,1,0:T(8,128)(2,1)} %pack.1), calls=%async_computation | async-start | bytes 4194304 | tf_op jit(solution)/shard_map/all_to_all | solution.py:459
  10.8 4.2 %slot_order.1 = (f32[16,2048]{1,0:T(8,128)S(1)}, f32[32,256]{1,0:T(8,128)S(1)}, f32[32,128]{1,0:T(8,128)S(1)}, bf16[256,2048]{1,0:T(8,128)(2,1)S(1)}, bf16[256,2...) custom-call(s32[1]{0:T(128)} %bitcast.mine_ref, s32[2,1024]{1,0:T(2,128)S(1)} %bitcast.9, s32[1,1024]{1,0:T(1,128)S(1)} %bitcast.10, ...), custom_call_target="tpu_custom_call" | custom-call | flops 4000000000 | bytes 8000000 | tf_op jit(solution)/shard_map/slot_order/pallas_call | solution.py:499
  15.0 1.0 copy-done
  16.0 1.0 copy-done.2
  17.0 20.2 %all-to-all-done.cells_ref = bf16[8,8,128,128]{3,2,1,0:T(8,128)(2,1)} async-done(((bf16[8,8,128,128]{3,2,1,0:T(8,128)(2,1)}), bf16[8,8,128,128]{3,2,1,0:T(8,128)(2,1)}, u32[]{:S(2)}, u32[]{:S(2)}) %all-to-all-start) | async-done | bytes 2097184 | tf_op jit(solution)/shard_map/all_to_all | solution.py:459
  37.2 1.3 %fusion = (bf16[2,4,128,128]{3,2,1,0:T(8,128)(2,1)S(1)}, bf16[2,4,128,128]{3,2,1,0:T(8,128)(2,1)S(1)}, bf16[2,4,128,128]{3,2,1,0:T(8,128)(2,1)S(1)}, bf16[2,4,128,128]{3,2,1,0:T(8,128)(2,1)S(1)}) fusion(bf16[8,8,128,128]{3,2,1,0:T(8,128)(2,1)} %all-to-all-done.cells_ref), kind=kLoop, calls=%fused_computation.1 | loop fusion | bytes 2097152 | tf_op jit(solution)/shard_map/slice | solution.py:603
  38.6 4.0 %collective-permute-start = (bf16[2,4,128,128]{3,2,1,0:T(8,128)(2,1)S(1)}, bf16[2,4,128,128]{3,2,1,0:T(8,128)(2,1)S(1)}, u32[]{:S(2)}, u32[]{:S(2)}) collective-permute-start(bf16[2,4,128,128]{3,2,1,0:T(8,128)(2,1)S(1)} %get-tuple-element.48), channel_id=1, source_target_pairs={{0,224},{4,228},{8,232},{12,236},{16,240},{20,244},{24,248},{28,25... | collective-permute-start | bytes 786440 | tf_op jit(solution)/shard_map/ppermute | solution.py:606
  42.7 5.5 %coherence.1 = (f32[8,96,128]{2,1,0:T(8,128)S(1)}, f32[16,128]{1,0:T(8,128)S(1)}, bf16[1024,640]{1,0:T(8,128)(2,1)S(1)}) custom-call(bf16[8,8,128,128]{3,2,1,0:T(8,128)(2,1)} %all-to-all-done.cells_ref, bf16[1024,640]{1,0:T(8,128)(2,1)S(1)} %copy-done.9), custom_call_target="tpu_custom_call" | custom-call | flops 4000000000 | bytes 8000000 | tf_op jit(solution)/shard_map/coherence/pallas_call | solution.py:518
  48.2 0.8 collective-permute-done.1.before_ref
  49.0 2.7 %edge.1 = (f32[8,128,128]{2,1,0:T(8,128)}, f32[32,128]{1,0:T(8,128)S(1)}) custom-call(bf16[2,4,128,128]{3,2,1,0:T(8,128)(2,1)S(1)} %get-tuple-element.49.last_ref, bf16[2,4,128,128]{3,2,1,0:T(8,128)(2,1)S(1)} %collective-permute-done.next_ref, bf16[2,4,128,128]{3,2,1,0:T(8,128)(2,1)S(1)} %collective-permute-done.1.before_ref, ...), custom_call_target="tpu_custom_call" | custom-call | flops 2000000000 | bytes 4000000 | tf_op jit(solution)/shard_map/edge/pallas_call | solution.py:539
  51.6 5.0 %all-to-all-start.1 = ((f32[8,128,128]{2,1,0:T(8,128)}), f32[8,128,128]{2,1,0:T(8,128)S(1)}, u32[]{:S(2)}, u32[]{:S(2)}) async-start(f32[8,128,128]{2,1,0:T(8,128)} %get-tuple-element.33), calls=%async_computation.1 | async-start | bytes 1048576 | tf_op jit(solution)/shard_map/all_to_all | solution.py:459
  56.6 1.7 %collective-permute-start.2 = (f32[32,128]{1,0:T(8,128)S(1)}, f32[32,128]{1,0:T(8,128)S(1)}, u32[]{:S(2)}, u32[]{:S(2)}) collective-permute-start(f32[32,128]{1,0:T(8,128)S(1)} %get-tuple-element.35), channel_id=1, source_target_pairs={{0,4},{4,0},{8,12},{12,8},{16,20},{20,16},{24,28},{28,24},{32,36},... | collective-permute-start | bytes 49160 | tf_op jit(solution)/shard_map/ppermute | solution.py:468
  58.3 0.8 collective-permute-done.2
  59.2 2.5 %collective-permute-start.5 = (f32[32,128]{1,0:T(8,128)S(1)}, f32[32,128]{1,0:T(8,128)S(1)}, u32[]{:S(2)}, u32[]{:S(2)}) collective-permute-start(f32[32,128]{1,0:T(8,128)S(1)} %add.12), channel_id=1, source_target_pairs={{0,3},{1,2},{2,1},{3,0},{4,7},{5,6},{6,5},{7,4},{8,11},{9,10},{10,... | collective-permute-start | bytes 49160 | tf_op jit(solution)/shard_map/ppermute | solution.py:468
  62.4 0.5 collective-permute-done.5
  63.0 2.9 %collective-permute-done.4 = f32[32,128]{1,0:T(8,128)S(1)} collective-permute-done((f32[32,128]{1,0:T(8,128)S(1)}, f32[32,128]{1,0:T(8,128)S(1)}, u32[]{:S(2)}, u32[]{:S(2)}) %collective-permute-start.4) | collective-permute-done | bytes 16416 | tf_op jit(solution)/shard_map/ppermute | solution.py:468
  65.9 3.7 %all-to-all-done.1.table_ref = f32[8,128,128]{2,1,0:T(8,128)S(1)} async-done(((f32[8,128,128]{2,1,0:T(8,128)}), f32[8,128,128]{2,1,0:T(8,128)S(1)}, u32[]{:S(2)}, u32[]{:S(2)}) %all-to-all-start.1) | async-done | bytes 524320 | tf_op jit(solution)/shard_map/all_to_all | solution.py:459
  69.6 2.4 %select.1 = f32[1216,128]{1,0:T(8,128)} custom-call(s32[1]{0:T(128)} %bitcast.mine_ref, f32[8,128,128]{2,1,0:T(8,128)S(1)} %all-to-all-done.1.table_ref, f32[16,2048]{1,0:T(8,128)S(1)} %get-tuple-element.34.code_ref, f32[32,128]{1,0:T(8,128)S(1)} %add_add_fusion.sum_ref), custom_call_target="tpu_custom_call" | custom-call | flops 2000000000 | bytes 4000000 | tf_op jit(solution)/shard_map/select/pallas_call | solution.py:559
  72.0 8.3 %all-to-all-start.2 = ((f32[64,1,2432]{2,1,0:T(1,128)}), f32[64,1,2432]{2,1,0:T(1,128)S(1)}, u32[]{:S(2)}, u32[]{:S(2)}) async-start(f32[64,1,2432]{2,1,0:T(1,128)} %bitcast.4), calls=%async_computation.2 | async-start | bytes 1245184 | tf_op jit(solution)/shard_map/all_to_all | solution.py:459
  80.4 3.4 %series.1.series_in_ref = f32[64,256]{1,0:T(8,128)} custom-call(s32[1]{0:T(128)} %bitcast.mine_ref, f32[8,128,128]{2,1,0:T(8,128)} %copy-done.4, bf16[256,2048]{1,0:T(8,128)(2,1)} %copy-done, bf16[256,2048]{1,0:T(8,128)(2,1)} %copy-done.2), custom_call_target="tpu_custom_call" | custom-call | flops 1000000000 | bytes 3000000 | tf_op jit(solution)/shard_map/series/pallas_call | solution.py:571
  83.7 16.3 %all-to-all-done.2 = f32[64,1,2432]{2,1,0:T(1,128)S(1)} async-done(((f32[64,1,2432]{2,1,0:T(1,128)}), f32[64,1,2432]{2,1,0:T(1,128)S(1)}, u32[]{:S(2)}, u32[]{:S(2)}) %all-to-all-start.2) | async-done | bytes 622624 | tf_op jit(solution)/shard_map/all_to_all | solution.py:459
  100.1 0.8 copy-done.5
  100.9 1.9 %referenced.1 = (f32[64,256]{1,0:T(8,128)}, f32[1024,128]{1,0:T(8,128)}) custom-call(f32[1216,128]{1,0:T(8,128)S(1)} %bitcast.8, bf16[256,2048]{1,0:T(8,128)(2,1)S(1)} %copy-done.1, bf16[256,2048]{1,0:T(8,128)(2,1)S(1)} %copy-done.3, f32[32,256]{1,0:T(8,128)S(1)} %get-tuple-element.38.own_early_ref, f32[32,128]{1,0:T(8,128)S(1)} %get-tuple-element.39.own_lag_ref, ...), custom_call_target="tpu_custom_call" | custom-call | tf_op jit(solution)/shard_map/referenced/pallas_call | solution.py:583
  (24 shorter events, 1.0 us)
Async XLA Ops:
  3.2 7.7 %copy-start.6 = (f32[256,1024]{1,0:T(8,128)S(1)}, f32[256,1024]{1,0:T(8,128)}, u32[]{:S(2)}) copy-start(f32[256,1024]{1,0:T(8,128)} %pinv_ref.1) | copy-start | bytes 3145732
  3.2 7.7 %copy-start.7 = (s32[1024,2]{0,1:T(2,128)S(1)}, s32[1024,2]{0,1:T(2,128)}, u32[]{:S(2)}) copy-start(s32[1024,2]{0,1:T(2,128)} %param.5) | copy-start | bytes 24580
  3.2 7.7 %copy-start.8 = (s32[1024,1]{0,1:T(1,128)S(1)}, s32[1024,1]{0,1:T(1,128)}, u32[]{:S(2)}) copy-start(s32[1024,1]{0,1:T(1,128)} %param.6) | copy-start | bytes 12292
  3.2 34.0 %all-to-all-start = ((bf16[8,8,128,128]{3,2,1,0:T(8,128)(2,1)}), bf16[8,8,128,128]{3,2,1,0:T(8,128)(2,1)}, u32[]{:S(2)}, u32[]{:S(2)}) async-start(bf16[8,8,128,128]{3,2,1,0:T(8,128)(2,1)} %pack.1), calls=%async_computation | async-start | bytes 4194304 | tf_op jit(solution)/shard_map/all_to_all | solution.py:459
  15.0 1.0 copy-start
  16.0 1.0 copy-start.2
  17.0 25.7 %copy-start.9 = (bf16[1024,640]{1,0:T(8,128)(2,1)S(1)}, bf16[1024,640]{1,0:T(8,128)(2,1)}, u32[]{:S(2)}) copy-start(bf16[1024,640]{1,0:T(8,128)(2,1)} %get-tuple-element.29.table_ref) | copy-start | bytes 3932164
  38.4 10.5 %collective-permute-start.1 = (bf16[2,4,128,128]{3,2,1,0:T(8,128)(2,1)S(1)}, bf16[2,4,128,128]{3,2,1,0:T(8,128)(2,1)S(1)}, u32[]{:S(2)}, u32[]{:S(2)}) collective-permute-start(bf16[2,4,128,128]{3,2,1,0:T(8,128)(2,1)S(1)} %get-tuple-element.47), channel_id=1, source_target_pairs={{0,32},{4,36},{8,40},{12,44},{16,48},{20,52},{24,56},{28,60},{32,6... | collective-permute-start | bytes 786440 | tf_op jit(solution)/shard_map/ppermute | solution.py:607
  38.6 10.3 %collective-permute-start = (bf16[2,4,128,128]{3,2,1,0:T(8,128)(2,1)S(1)}, bf16[2,4,128,128]{3,2,1,0:T(8,128)(2,1)S(1)}, u32[]{:S(2)}, u32[]{:S(2)}) collective-permute-start(bf16[2,4,128,128]{3,2,1,0:T(8,128)(2,1)S(1)} %get-tuple-element.48), channel_id=1, source_target_pairs={{0,224},{4,228},{8,232},{12,236},{16,240},{20,244},{24,248},{28,25... | collective-permute-start | bytes 786440 | tf_op jit(solution)/shard_map/ppermute | solution.py:606
  51.6 18.0 %all-to-all-start.1 = ((f32[8,128,128]{2,1,0:T(8,128)}), f32[8,128,128]{2,1,0:T(8,128)S(1)}, u32[]{:S(2)}, u32[]{:S(2)}) async-start(f32[8,128,128]{2,1,0:T(8,128)} %get-tuple-element.33), calls=%async_computation.1 | async-start | bytes 1048576 | tf_op jit(solution)/shard_map/all_to_all | solution.py:459
  56.6 2.6 %collective-permute-start.2 = (f32[32,128]{1,0:T(8,128)S(1)}, f32[32,128]{1,0:T(8,128)S(1)}, u32[]{:S(2)}, u32[]{:S(2)}) collective-permute-start(f32[32,128]{1,0:T(8,128)S(1)} %get-tuple-element.35), channel_id=1, source_target_pairs={{0,4},{4,0},{8,12},{12,8},{16,20},{20,16},{24,28},{28,24},{32,36},... | collective-permute-start | bytes 49160 | tf_op jit(solution)/shard_map/ppermute | solution.py:468
  59.2 3.8 %collective-permute-start.5 = (f32[32,128]{1,0:T(8,128)S(1)}, f32[32,128]{1,0:T(8,128)S(1)}, u32[]{:S(2)}, u32[]{:S(2)}) collective-permute-start(f32[32,128]{1,0:T(8,128)S(1)} %add.12), channel_id=1, source_target_pairs={{0,3},{1,2},{2,1},{3,0},{4,7},{5,6},{6,5},{7,4},{8,11},{9,10},{10,... | collective-permute-start | bytes 49160 | tf_op jit(solution)/shard_map/ppermute | solution.py:468
  61.7 4.2 %collective-permute-start.4 = (f32[32,128]{1,0:T(8,128)S(1)}, f32[32,128]{1,0:T(8,128)S(1)}, u32[]{:S(2)}, u32[]{:S(2)}) collective-permute-start(f32[32,128]{1,0:T(8,128)S(1)} %add.12), channel_id=1, source_target_pairs={{0,2},{1,3},{2,0},{3,1},{4,6},{5,7},{6,4},{7,5},{8,10},{9,11},{10,... | collective-permute-start | bytes 49160 | tf_op jit(solution)/shard_map/ppermute | solution.py:468
  62.2 3.7 %collective-permute-start.3 = (f32[32,128]{1,0:T(8,128)S(1)}, f32[32,128]{1,0:T(8,128)S(1)}, u32[]{:S(2)}, u32[]{:S(2)}) collective-permute-start(f32[32,128]{1,0:T(8,128)S(1)} %add.12), channel_id=1, source_target_pairs={{0,1},{1,0},{2,3},{3,2},{4,5},{5,4},{6,7},{7,6},{8,9},{9,8},{10,11... | collective-permute-start | bytes 49160 | tf_op jit(solution)/shard_map/ppermute | solution.py:468
  69.6 2.4 %copy-start.4 = (f32[8,128,128]{2,1,0:T(8,128)}, f32[8,128,128]{2,1,0:T(8,128)S(1)}, u32[]{:S(2)}) copy-start(f32[8,128,128]{2,1,0:T(8,128)S(1)} %all-to-all-done.1.table_ref) | copy-start | bytes 1572868
  72.0 28.0 %all-to-all-start.2 = ((f32[64,1,2432]{2,1,0:T(1,128)}), f32[64,1,2432]{2,1,0:T(1,128)S(1)}, u32[]{:S(2)}, u32[]{:S(2)}) async-start(f32[64,1,2432]{2,1,0:T(1,128)} %bitcast.4), calls=%async_computation.2 | async-start | bytes 1245184 | tf_op jit(solution)/shard_map/all_to_all | solution.py:459
  80.3 19.7 %copy-start.1 = (bf16[256,2048]{1,0:T(8,128)(2,1)S(1)}, bf16[256,2048]{1,0:T(8,128)(2,1)}, u32[]{:S(2)}) copy-start(bf16[256,2048]{1,0:T(8,128)(2,1)} %copy-done) | copy-start | bytes 3145732
  80.4 19.7 %copy-start.3 = (bf16[256,2048]{1,0:T(8,128)(2,1)S(1)}, bf16[256,2048]{1,0:T(8,128)(2,1)}, u32[]{:S(2)}) copy-start(bf16[256,2048]{1,0:T(8,128)(2,1)} %copy-done.2) | copy-start | bytes 3145732
  100.1 0.8 copy-start.5
